TPU v7x, 128 devices: a whole 4x4x4 slice. The times are simulated.
128 devices in a mesh: col: 16 (over x, y), obs: 8 (over z, core).
Axes of the slice: x: 4, y: 4, z: 4, core: 2. Of those that a mesh axis runs over, the one named last changes fastest.
Arguments:
- departures: float32 [16384, 4096], P(('col', 'obs')), may hold values from -6 to 6
- obs_owner: int32 [16384, 1], P(('col', 'obs')), may hold values from 0 to 127; in each aligned block of 128 rows (0 to 127, 128 to 255, ...) at most 2 rows name the same one
- obs_column: int32 [16384], P(('col', 'obs')), may hold values from 0 to 1023
- obs_count: int32 [128], P(('col', 'obs')), may hold values from 64 to 128, as said below
- channel_count: int32 [8], P('obs'), may hold values from 256 to 4096, as said below
- error_inv: float32 [8, 4096], P('obs'), may hold values from 0.25 to 4
- jacobian: bfloat16 [8, 548, 4096], P('obs'), may hold values from -0.25 to 0.25
- vertical: float32 [4, 137, 137], replicated, may hold values from -0.5 to 0.5
Outputs:
- increment: float32 [4, 137, 131072], P(None, None, ('col', 'obs'))
- residual: float32 [4, 137, 131072], P(None, None, ('col', 'obs'))
Inputs may be any that keep to these rules, and one draw needn't show every extreme that they name: `obs_owner`: within the rows of one device (aligned blocks of 128 rows) no owner is named by more than 2 rows; in some block some owner is named by exactly 2. `obs_count`: some device uses all 128 slots. `channel_count`: some swath uses all 4096 channels.
All inputs are finite; a program needn't handle non-finite values.
Results may differ from a plain program's by a relative error of at most 0.017.
Values may be sent and summed in bfloat16 or wider, within the bound.
A program may use at most 64 MiB of HBM per device.

v0:
```python
import jax
import jax.numpy as jnp
from jax import lax
from jax.sharding import PartitionSpec as P

COLS_DEV = 1024
ITERS = 2


def per_device(
    departures, obs_owner, obs_column, obs_count, channel_count, error_inv, jacobian, vertical
):
    obs_rows, channels = departures.shape
    var_count, levels, _ = vertical.shape
    features = var_count * levels
    device_count = lax.axis_size(("col", "obs"))
    capacity = max(2, (2 * obs_rows + device_count - 1) // device_count)
    owner_index = obs_owner[:, 0]
    owner_hits = (
        owner_index[:, None] == jnp.arange(device_count, dtype=jnp.int32)[None, :]
    ).astype(jnp.int32)
    bucket_slot = jnp.sum(jnp.cumsum(owner_hits, axis=0) * owner_hits, axis=1) - 1
    flat_index = owner_index * capacity + bucket_slot
    asked = jnp.zeros((device_count * capacity,), jnp.int32).at[flat_index].set(obs_column)
    incoming = lax.all_to_all(
        asked.reshape(device_count, capacity),
        ("col", "obs"),
        split_axis=0,
        concat_axis=0,
        tiled=True,
    ).reshape(-1)
    jac_swath = jacobian[0]
    weights_inv = error_inv[0]
    channel_live = channel_count[0]
    live_mask = (jnp.arange(obs_rows, dtype=jnp.int32) < obs_count[0])[:, None] & (
        jnp.arange(channels, dtype=jnp.int32) < channel_live
    )[None, :]
    contract = (((1,), (1,)), ((), ()))

    def backward(adjoint_rows, columns_here):
        outgoing = (
            jnp.zeros((device_count * capacity, features), jnp.float32)
            .at[flat_index]
            .set(adjoint_rows)
        )
        outgoing = outgoing.reshape(device_count, capacity, features)
        returned = lax.all_to_all(
            outgoing.astype(jnp.bfloat16), ("col", "obs"), split_axis=0, concat_axis=0, tiled=True
        ).astype(outgoing.dtype)
        summed = (
            jnp.zeros((columns_here, features), jnp.float32)
            .at[incoming]
            .add(returned.reshape(device_count * capacity, features))
        )
        spread = summed.T.reshape(var_count, levels, columns_here)
        return jnp.einsum("aij,aic->ajc", vertical, spread, precision=lax.Precision.HIGHEST)

    def adjoint_of(evolved):
        weighted = (weights_inv[None, :] * evolved).astype(jnp.bfloat16)
        return lax.dot_general(weighted, jac_swath, contract, preferred_element_type=jnp.float32)

    def squares(field):
        return lax.psum(jnp.sum(field * field), ("col", "obs"))

    rhs = backward(adjoint_of(jnp.where(live_mask, departures, jnp.float32(0.0))), COLS_DEV)
    increment = jnp.zeros_like(rhs)
    residual = rhs
    direction = rhs
    norm_now = squares(residual)
    for iteration in range(ITERS):
        forward_columns_here = direction.shape[2]
        lifted = jnp.einsum("aij,ajc->aic", vertical, direction, precision=lax.Precision.HIGHEST)
        packed = lifted.reshape(features, forward_columns_here).astype(jnp.bfloat16)
        forward_outgoing = jnp.take(packed, incoming, axis=1).T.reshape(
            device_count, capacity, features
        )
        arrived = lax.all_to_all(
            forward_outgoing, ("col", "obs"), split_axis=0, concat_axis=0, tiled=True
        )
        tangent_evolved = jnp.dot(
            arrived.reshape(device_count * capacity, features)[flat_index],
            jac_swath,
            preferred_element_type=jnp.float32,
        )
        applied = direction + backward(
            adjoint_of(jnp.where(live_mask, tangent_evolved, jnp.float32(0.0))), direction.shape[2]
        )
        step_length = norm_now / lax.psum(jnp.sum(direction * applied), ("col", "obs"))
        increment = increment + step_length * direction
        residual = residual - step_length * applied
        norm_next = squares(residual)
        direction = residual + norm_next / norm_now * direction
        norm_now = norm_next
    return (increment, residual)


def solution(mesh):
    in_specs = (
        P(("col", "obs"), None),
        P(("col", "obs"), None),
        P(("col", "obs")),
        P(("col", "obs")),
        P("obs"),
        P("obs", None),
        P("obs", None, None),
        P(),
    )
    out_specs = (P(None, None, ("col", "obs")), P(None, None, ("col", "obs")))
    return jax.shard_map(
        per_device, mesh=mesh, in_specs=in_specs, out_specs=out_specs, check_vma=False
    )
```

profile of v0, /device:TPU:0, one launch (start us, length us, event | category | flops | bytes accessed | tf_op | source)
XLA Modules:
  0.0 424.8 jit_solution(12575353637768950690)
XLA Ops:
  4.9 11.1 %all-to-all-start = ((s32[128,1,2]{2,1,0:T(1,128)}), s32[128,1,2]{2,1,0:T(1,128)S(1)}, u32[]{:S(2)}, u32[]{:S(2)}) async-start(s32[128,1,2]{2,1,0:T(1,128)} %bitcast.3), calls=%async_computation | async-start | bytes 131072 | tf_op jit(solution)/shard_map/all_to_all | solution.py:25
  17.4 4.7 %fusion.10 = f32[128,548]{1,0:T(8,128)S(1)} fusion(bf16[1,548,4096]{2,1,0:T(8,128)(2,1)} %param.16, f32[128,4096]{1,0:T(8,128)} %param.10, f32[4096]{0:T(1024)} %bitcast.117, pred[4096]{0:T(1024)(128)(4,1)S(1)} %iota_compare_fusion.1, pred[128]{0:T(512)(128)(4,1)S(1)} %iota_compare_fusion.2), kind=kOutput, calls=%fused_computation.23 | convolution fusion | flops 576716800 | bytes 6887552 | tf_op jit(solution)/shard_map/dot_general | solution.py:60
  22.1 1.2 scatter_custom_fusion.1
  25.5 8.8 %all-to-all-start.1 = ((bf16[128,2,548]{2,1,0:T(2,128)(2,1)}), bf16[128,2,548]{2,1,0:T(2,128)(2,1)S(1)}, u32[]{:S(2)}, u32[]{:S(2)}) async-start(bf16[128,2,548]{2,1,0:T(2,128)(2,1)} %convert_element_type.54), calls=%async_computation.1 | async-start | bytes 655360 | tf_op jit(solution)/shard_map/all_to_all | solution.py:47
  36.0 10.0 %all-to-all-done.1 = bf16[128,2,548]{2,1,0:T(2,128)(2,1)S(1)} async-done(((bf16[128,2,548]{2,1,0:T(2,128)(2,1)}), bf16[128,2,548]{2,1,0:T(2,128)(2,1)S(1)}, u32[]{:S(2)}, u32[]{:S(2)}) %all-to-all-start.1) | async-done | bytes 280608 | tf_op jit(solution)/shard_map/all_to_all | solution.py:47
  46.2 4.0 scatter_custom_fusion.2
  50.2 2.1 copy.36
  52.3 1.7 reshape.117
  54.0 3.8 fusion.59
  57.8 3.3 fusion.22
  61.1 2.6 convert_element_type.57
  63.7 2.4 copy.39
  66.0 3.5 gather_fusion.2
  71.5 5.7 %all-to-all-start.2 = ((bf16[128,2,548]{2,1,0:T(2,128)(2,1)}), bf16[128,2,548]{2,1,0:T(2,128)(2,1)}, u32[]{:S(2)}, u32[]{:S(2)}) async-start(bf16[128,2,548]{2,1,0:T(2,128)(2,1)} %reshape.119), calls=%async_computation.2 | async-start | bytes 655360 | tf_op jit(solution)/shard_map/all_to_all | solution.py:77
  77.2 11.3 %all-to-all-done.2 = bf16[128,2,548]{2,1,0:T(2,128)(2,1)} async-done(((bf16[128,2,548]{2,1,0:T(2,128)(2,1)}), bf16[128,2,548]{2,1,0:T(2,128)(2,1)}, u32[]{:S(2)}, u32[]{:S(2)}) %all-to-all-start.2) | async-done | bytes 280608 | tf_op jit(solution)/shard_map/all_to_all | solution.py:77
  88.5 1.2 reshape.120
  90.6 6.4 %fusion.7 = f32[128,548]{1,0:T(8,128)S(1)} fusion(bf16[1,548,4096]{2,1,0:T(8,128)(2,1)} %param.16, bf16[128,548]{1,0:T(8,128)(2,1)S(1)} %gather_fusion, f32[4096]{0:T(1024)S(1)} %bitcast.118, pred[4096]{0:T(1024)(128)(4,1)S(1)} %iota_compare_fusion.1, pred[128]{0:T(512)(128)(4,1)S(1)} %iota_compare_fusion.2), kind=kOutput, calls=%fused_computation.20 | convolution fusion | flops 1151336448 | bytes 4930688 | tf_op jit(solution)/shard_map/dot_general | solution.py:60
  97.0 1.8 scatter_custom_fusion.3
  98.8 1.8 convert_element_type.59
  100.7 1.1 convert_element_type.60
  101.8 16.5 %all_to_all.34 = bf16[128,2,548]{2,1,0:T(2,128)(2,1)} all-to-all(bf16[128,2,548]{2,1,0:T(2,128)(2,1)S(1)} %convert_element_type.60), channel_id=1, replica_groups=mesh['col'=16,'obs'=8] {'col','obs'}, dimensions={0} | all-to-all | bytes 561152 | tf_op jit(solution)/shard_map/all_to_all | solution.py:47
  118.3 2.0 reshape.203
  120.3 4.4 %scatter_custom_fusion.4 = f32[1024,548]{1,0:T(8,128)} fusion(s32[256]{0:T(256)S(1)} %bitcast.123, f32[256,548]{1,0:T(8,128)} %reshape.203, f32[]{:T(128)} %constant.14.clone.1), kind=kCustom, calls=%fused_computation.48 | custom fusion | flops 140288 | bytes 2245120 | tf_op jit(solution)/shard_map/scatter-add | solution.py:53
  124.7 3.1 copy.41
  127.8 3.3 reshape.123
  131.1 6.3 %fusion.13 = (f32[]{:T(128)}, f32[]{:T(128)}, f32[4,1024,137]{1,2,0:T(8,128)}) fusion(f32[4,1024,137]{1,2,0:T(8,128)S(1)} %fusion.59, f32[4,137,1024]{2,1,0:T(8,128)} %reshape.123, f32[4,137,137]{1,2,0:T(8,128)S(1)} %copy.37), kind=kOutput, calls=%fused_computation.34 | convolution fusion | flops 925339648 | bytes 7034136 | tf_op jit(solution)/shard_map/aij,aic->ajc/dot_general | solution.py:56
  137.4 62.9 %all-reduce = (f32[]{:T(128)}, f32[]{:T(128)}) all-reduce(f32[]{:T(128)} %get-tuple-element.10, f32[]{:T(128)} %get-tuple-element.9), channel_id=1, replica_groups=mesh['col'=16,'obs'=8] {'col','obs'}, use_global_device_ids=true, to_apply=%region_6.7 | all-reduce | flops 2 | bytes 16 | tf_op jit(solution)/shard_map/psum | solution.py:63
  201.6 2.9 multiply_reduce_fusion.1
  204.5 62.6 %psum.30 = f32[]{:T(128)} all-reduce(f32[]{:T(128)} %multiply_reduce_fusion.1), channel_id=1, replica_groups=mesh['col'=16,'obs'=8] {'col','obs'}, use_global_device_ids=true, to_apply=%region_12.14 | all-reduce | flops 1 | bytes 8 | tf_op jit(solution)/shard_map/psum | solution.py:63
  268.4 5.4 %fusion.23 = bf16[4,137,1024]{2,1,0:T(8,128)(2,1)} fusion(f32[4,137,137]{2,0,1:T(4,128)S(1)} %copy-done.1, f32[4,1024,137]{1,2,0:T(8,128)S(1)} %fusion.59, f32[]{:T(128)S(6)} %div.10, f32[4,1024,137]{1,2,0:T(8,128)} %get-tuple-element.15, f32[]{:T(128)S(6)} %div.9), kind=kOutput, calls=%fused_computation.45 | convolution fusion | flops 925900800 | bytes 5911832 | tf_op jit(solution)/shard_map/aij,ajc->aic/dot_general | solution.py:72
  273.8 2.6 convert_element_type.63
  276.3 2.4 copy.44
  278.7 3.5 gather_fusion.3
  284.2 17.7 %all_to_all.35 = bf16[128,2,548]{2,1,0:T(2,128)(2,1)} all-to-all(bf16[128,2,548]{2,1,0:T(2,128)(2,1)} %reshape.124), channel_id=1, replica_groups=mesh['col'=16,'obs'=8] {'col','obs'}, dimensions={0} | all-to-all | bytes 561152 | tf_op jit(solution)/shard_map/all_to_all | solution.py:77
  301.9 1.2 reshape.125
  304.0 6.4 %fusion.4 = f32[128,548]{1,0:T(8,128)S(1)} fusion(bf16[1,548,4096]{2,1,0:T(8,128)(2,1)} %param.16, bf16[128,548]{1,0:T(8,128)(2,1)S(1)} %gather_fusion.1, f32[4096]{0:T(1024)S(1)} %bitcast.119, pred[4096]{0:T(1024)(128)(4,1)S(1)} %iota_compare_fusion.1, pred[128]{0:T(512)(128)(4,1)S(1)} %iota_compare_fusion.2), kind=kOutput, calls=%fused_computation.17 | convolution fusion | flops 1151336448 | bytes 4930688 | tf_op jit(solution)/shard_map/dot_general | solution.py:60
  310.4 1.8 scatter_custom_fusion.5
  312.3 1.8 convert_element_type.65
  315.2 16.5 %all_to_all.36 = bf16[128,2,548]{2,1,0:T(2,128)(2,1)} all-to-all(bf16[128,2,548]{2,1,0:T(2,128)(2,1)S(1)} %convert_element_type.66), channel_id=1, replica_groups=mesh['col'=16,'obs'=8] {'col','obs'}, dimensions={0} | all-to-all | bytes 561152 | tf_op jit(solution)/shard_map/all_to_all | solution.py:47
  331.7 2.0 reshape.219
  333.7 4.4 %scatter_custom_fusion.6 = f32[1024,548]{1,0:T(8,128)} fusion(s32[256]{0:T(256)S(1)} %bitcast.124, f32[256,548]{1,0:T(8,128)} %reshape.219, f32[]{:T(128)} %constant.14.clone.1), kind=kCustom, calls=%fused_computation.46 | custom fusion | flops 140288 | bytes 2245120 | tf_op jit(solution)/shard_map/scatter-add | solution.py:53
  338.1 3.1 copy.46
  341.2 3.3 reshape.128
  344.6 7.2 %multiply_reduce_fusion = (f32[]{:T(128)}, f32[4,1024,137]{1,2,0:T(8,128)}) fusion(f32[]{:T(128)S(6)} %div.10, f32[4,1024,137]{1,2,0:T(8,128)} %get-tuple-element.15, f32[]{:T(128)S(6)} %div.9, f32[4,1024,137]{1,2,0:T(8,128)S(1)} %fusion.59, f32[4,137,1024]{2,1,0:T(8,128)} %reshape.128, f32[4,137,137]{1,2,0:T(8,128)S(1)} %copy.37), kind=kOutput, calls=%fused_computation.38 | convolution fusion | flops 927023104 | bytes 9278748 | tf_op jit(solution)/shard_map/aij,aic->ajc/dot_general | solution.py:56
  351.7 62.8 %psum.31 = f32[]{:T(128)} all-reduce(f32[]{:T(128)} %get-tuple-element.16), channel_id=1, replica_groups=mesh['col'=16,'obs'=8] {'col','obs'}, use_global_device_ids=true, to_apply=%region_16.18 | all-reduce | flops 1 | bytes 8 | tf_op jit(solution)/shard_map/psum | solution.py:88
  415.8 3.3 multiply_subtract_fusion
  419.0 2.8 copy.49
  421.8 2.8 copy.48
  (35 shorter events, 15.1 us)
Async XLA Ops:
  4.9 20.6 %all-to-all-start = ((s32[128,1,2]{2,1,0:T(1,128)}), s32[128,1,2]{2,1,0:T(1,128)S(1)}, u32[]{:S(2)}, u32[]{:S(2)}) async-start(s32[128,1,2]{2,1,0:T(1,128)} %bitcast.3), calls=%async_computation | async-start | bytes 131072 | tf_op jit(solution)/shard_map/all_to_all | solution.py:25
  22.1 2.1 copy-start
  25.5 20.5 %all-to-all-start.1 = ((bf16[128,2,548]{2,1,0:T(2,128)(2,1)}), bf16[128,2,548]{2,1,0:T(2,128)(2,1)S(1)}, u32[]{:S(2)}, u32[]{:S(2)}) async-start(bf16[128,2,548]{2,1,0:T(2,128)(2,1)} %convert_element_type.54), calls=%async_computation.1 | async-start | bytes 655360 | tf_op jit(solution)/shard_map/all_to_all | solution.py:47
  69.5 21.1 %copy-start.2 = (f32[1,4096]{1,0:T(1,128)S(1)}, f32[1,4096]{1,0:T(1,128)}, u32[]{:S(2)}) copy-start(f32[1,4096]{1,0:T(1,128)} %param.15) | copy-start | bytes 49156
  71.5 17.0 %all-to-all-start.2 = ((bf16[128,2,548]{2,1,0:T(2,128)(2,1)}), bf16[128,2,548]{2,1,0:T(2,128)(2,1)}, u32[]{:S(2)}, u32[]{:S(2)}) async-start(bf16[128,2,548]{2,1,0:T(2,128)(2,1)} %reshape.119), calls=%async_computation.2 | async-start | bytes 655360 | tf_op jit(solution)/shard_map/all_to_all | solution.py:77
  201.6 66.8 %copy-start.1 = (f32[4,137,137]{2,0,1:T(4,128)S(1)}, f32[4,137,137]{2,0,1:T(4,128)}, u32[]{:S(2)}) copy-start(f32[4,137,137]{2,0,1:T(4,128)} %param.17) | copy-start | bytes 900916
where the time goes:
time: 432 us; the launch traced here: 425 us
  blocking collectives  239 us (55%)
  local copies, waits for them, and re-layouts  60.3 us (14%)
  matrix products  43.3 us (10%)
  other arithmetic  28.1 us (7%)
  starting transfers between devices  25.6 us (6%)
  waiting for transfers between devices  22.2 us (5%)
  between operations  6.22 us (1%)
    psum x2, blocking collectives, squares(): return lax.psum(jnp.sum(field * field), ('col', 'obs'))  125 us
    psum x1, blocking collectives, per_device(): lax.psum(jnp.sum(direction * applied), ('col', 'obs'))  62.8 us
    all_to_all x2, blocking collectives, backward(): lax.all_to_all(outgoing.astype(jnp.bfloat16), ('col', 'obs'), split_axis=...  33 us
    all_to_all x1, blocking collectives, per_device(): lax.all_to_all(forward_outgoing, ('col', 'obs'), split_axis=0, concat_axi...  17.7 us
    dot_general x3, matrix products, adjoint_of(): lax.dot_general(weighted, jac_swath, contract, preferred_element_type=jnp...  17.4 us
    dot_general x3, matrix products, backward(): jnp.einsum('aij,aic->ajc', vertical, spread, precision=lax.Precision.HIGH...  17.3 us
    scatter-add x3, other arithmetic, backward(): summed = jnp.zeros((columns_here, features), jnp.float32).at[incoming].ad...  12.8 us
    all_to_all x1, waiting for transfers between devices, per_device(): lax.all_to_all(forward_outgoing, ('col', 'obs'), split_axis=0, concat_axi...  11.3 us
  transfers between devices with their start and end apart: 3, of which 3 were waited for; matrix products, arithmetic and copies ran while one was open for 2% of the time, Pallas kernels for 0%

commit v1 on v0

v1 whole, which is shorter than its diff:
```python
import jax
import jax.numpy as jnp
from jax import lax
from jax.experimental import pallas as pl
from jax.experimental.pallas import tpu as pltpu
from jax.sharding import PartitionSpec as P

MESH = pl.DeviceIdType.MESH
BF = jnp.bfloat16
F32 = jnp.float32
COLS_DEV = 1024
NVAR, LEV = 4, 137
FEAT = NVAR * LEV
FPAD = 640
ROWS = 128
SLOTS = 256
CH = 4096
CHUNK = 512
NCHUNK = CH // CHUNK
N_COL, N_OBS = 16, 8
COL_ROWS = SLOTS // N_COL
OBS_ROWS = SLOTS // N_OBS
NT = (((1,), (1,)), ((), ()))
OBS_ORDER = (4, 5, 3, 2, 6, 7, 1)


def iota(shape, axis):
    return lax.broadcasted_iota(jnp.int32, shape, axis)


def total(value):
    return jnp.sum(jnp.sum(value, axis=0, keepdims=True), axis=1, keepdims=True)


def inner_loop(
    obs_count, channel_count, owner, column, error_inv, vertical, dep_hbm, jac_hbm,
    out_inc, out_res, out_column,
    dep, jac, lift, gram, kern, kacc, racc, sent, held, queued, rows0, prof0, hprof0, hadj0, rows1, prof1, hprof1, hadj1,
    rows2, tile_a, tile_b, in_sem, col_send, col_recv, obs_send, obs_recv, sum_send, sum_recv,
):
    col, obs = lax.axis_index("col"), lax.axis_index("obs")

    def load(chunk):
        lanes = pl.ds(pl.multiple_of(chunk * CHUNK, CHUNK), CHUNK)
        return (
            pltpu.make_async_copy(jac_hbm.at[0, :, lanes], jac.at[chunk], in_sem.at[0, chunk]),
            pltpu.make_async_copy(dep_hbm.at[:, lanes], dep.at[chunk], in_sem.at[1, chunk]),
        )

    for chunk in range(NCHUNK):
        for copy in load(chunk):
            copy.start()

    barrier = pltpu.get_barrier_semaphore()
    for step in range(1, N_OBS):
        pl.semaphore_signal(barrier, inc=1, device_id={"obs": lax.rem(obs + step, N_OBS)}, device_id_type=MESH)
    for step in range(1, N_COL):
        pl.semaphore_signal(barrier, inc=1, device_id={"col": lax.rem(col + step, N_COL)}, device_id_type=MESH)

    lift[...] = jnp.zeros_like(lift)
    for var in range(NVAR):
        lift[var * LEV : (var + 1) * LEV, var * 256 : var * 256 + LEV] = vertical[var]
    gram[...] = jnp.zeros_like(gram)
    for var in range(NVAR):
        part = lift[var * 128 : var * 128 + 256, var * 256 : var * 256 + 256]
        square = lax.dot_general(part, part, NT, precision=lax.Precision.HIGHEST, preferred_element_type=F32)
        where = slice(var * 128, var * 128 + 256)
        gram[where, where] = gram[where, where] + square

    owner_lanes = jnp.broadcast_to(owner[...].astype(F32), (ROWS, ROWS))
    owner_rows = owner_lanes.T
    earlier = jnp.where((owner_lanes == owner_rows) & (iota((ROWS, ROWS), 0) < iota((ROWS, ROWS), 1)), 1.0, 0.0)
    slot = owner[...] * 2 + jnp.sum(earlier, axis=0, keepdims=True).astype(jnp.int32)
    live_lanes = iota((1, ROWS), 1) < obs_count[0]
    place = jnp.where((iota((SLOTS, ROWS), 0) == slot) & live_lanes, 1.0, 0.0).astype(BF)
    column_rows = jnp.broadcast_to(column[...].astype(F32), (ROWS, ROWS)).T[:, 0:1]
    column_high = jnp.floor(column_rows * (1.0 / 32.0))
    column_low = column_rows - 32.0 * column_high

    def weights(chunk):
        lanes = pl.ds(pl.multiple_of(chunk * CHUNK, CHUNK), CHUNK)
        channel = chunk * CHUNK + iota((1, CHUNK), 1)
        return jnp.where(channel < channel_count[0], error_inv[:, lanes], 0.0)

    racc[...] = jnp.zeros_like(racc)

    def rhs_chunk(chunk, carry):
        for copy in load(chunk):
            copy.wait()
        weighted = (weights(chunk) * dep[chunk]).astype(BF)
        racc[:, 0:FEAT] += lax.dot_general(weighted, jac[chunk], NT, preferred_element_type=F32)
        return carry

    lax.fori_loop(0, NCHUNK, rhs_chunk, 0)
    lane = iota((ROWS, FPAD), 1)
    rows = racc[...]
    rows = jnp.where(lane == FEAT, column_high, rows)
    rows = jnp.where(lane == FEAT + 1, column_low, rows)
    rows = jnp.where(lane == FEAT + 2, 1.0, rows)
    sent[...] = jnp.dot(place, rows.astype(BF), preferred_element_type=F32).astype(BF)

    pl.semaphore_wait(barrier, N_OBS - 1 + N_COL - 1)

    def block(index, size):
        return pl.ds(pl.multiple_of(index * size, size), size)

    col_copies = []
    for step in range(1, N_COL):
        other = lax.rem(col + step, N_COL)
        copy = pltpu.make_async_remote_copy(
            src_ref=sent.at[block(other, COL_ROWS)], dst_ref=held.at[block(col, COL_ROWS)],
            send_sem=col_send.at[step], recv_sem=col_recv.at[step],
            device_id={"col": other}, device_id_type=MESH,
        )
        copy.start()
        col_copies.append(copy)
    held[block(col, COL_ROWS), :] = sent[block(col, COL_ROWS), :]

    kacc[...] = jnp.zeros_like(kacc)

    def kern_chunk(chunk, carry):
        block_in = jac[chunk]
        scaled = (block_in.astype(F32) * weights(chunk)).astype(BF)
        kacc[0:FEAT, 0:FEAT] += lax.dot_general(scaled, block_in, NT, preferred_element_type=F32)
        return carry

    lax.fori_loop(0, NCHUNK, kern_chunk, 0)
    kern[...] = kacc[...].astype(BF)

    for copy in col_copies:
        copy.wait_recv()

    target, source = iota((SLOTS, SLOTS), 0), iota((SLOTS, SLOTS), 1)
    wanted = lax.rem(target // 2, N_COL) * COL_ROWS + (target // OBS_ROWS) * 2 + lax.rem(target, 2)
    turn = jnp.where(source == wanted, 1.0, 0.0).astype(BF)
    queued[...] = jnp.dot(turn, held[...], preferred_element_type=F32).astype(BF)

    def exchange(number, source_ref, target_ref):
        copies = []
        for step in OBS_ORDER:
            other = lax.rem(obs + step, N_OBS)
            copy = pltpu.make_async_remote_copy(
                src_ref=source_ref.at[block(other, OBS_ROWS)], dst_ref=target_ref.at[block(obs, OBS_ROWS)],
                send_sem=obs_send.at[number, step], recv_sem=obs_recv.at[number, step],
                device_id={"obs": other}, device_id_type=MESH,
            )
            copy.start()
            copies.append(copy)
        target_ref[block(obs, OBS_ROWS), :] = source_ref[block(obs, OBS_ROWS), :]
        return copies

    def arrive(copies):
        for copy in copies:
            copy.wait_recv()

    first = exchange(0, queued, rows0)
    arrive(first)

    extra = rows0[:, 512:640].astype(F32)
    extra_lanes = extra.T
    at = FEAT - 512
    live = extra[:, at + 2 : at + 3]
    column_of = jnp.where(live > 0.5, extra[:, at : at + 1] * 32.0 + extra[:, at + 1 : at + 2], -1.0)
    column_across = jnp.where(
        extra_lanes[at + 2 : at + 3, :] > 0.5,
        extra_lanes[at : at + 1, :] * 32.0 + extra_lanes[at + 1 : at + 2, :],
        -2.0,
    )
    same = jnp.where(column_of == column_across, 1.0, 0.0).astype(BF)
    out_column[...] = jnp.broadcast_to(column_of, (SLOTS, 128)).astype(jnp.int32)

    gram_low = gram[...].astype(BF)

    def profile(rows_ref):
        gathered = jnp.dot(same, rows_ref[...], preferred_element_type=F32)
        return jnp.dot(gathered.astype(BF), gram_low, preferred_element_type=F32)

    def apply_kern(in_ref, out_ref):
        adjoint = jnp.dot(in_ref[...], kern[...], preferred_element_type=F32)
        out_ref[...] = adjoint.astype(BF)
        return total(adjoint * in_ref[...].astype(F32))

    lifted = profile(rows0)
    prof0[...] = lifted.astype(BF)
    second = exchange(1, prof0, hprof0)
    moment0 = total(lifted * rows0[...].astype(F32))
    arrive(second)
    moment1 = apply_kern(hprof0, hadj0)
    third = exchange(2, hadj0, rows1)
    arrive(third)
    lifted = profile(rows1)
    prof1[...] = lifted.astype(BF)
    fourth = exchange(3, prof1, hprof1)
    moment2 = total(lifted * rows1[...].astype(F32))
    arrive(fourth)
    moment3 = apply_kern(hprof1, hadj1)

    row = iota((8, 128), 0)
    mine = jnp.where(row == 0, moment0, jnp.where(row == 1, moment1, jnp.where(row == 2, moment2, jnp.where(row == 3, moment3, 0.0))))
    tile_a[obs] = mine
    sums = []
    for step in OBS_ORDER:
        copy = pltpu.make_async_remote_copy(
            src_ref=tile_a.at[obs], dst_ref=tile_a.at[obs], send_sem=sum_send.at[step], recv_sem=sum_recv.at[step],
            device_id={"obs": lax.rem(obs + step, N_OBS)}, device_id_type=MESH,
        )
        copy.start()
        sums.append(copy)
    fifth = exchange(4, hadj1, rows2)
    for copy in sums:
        copy.wait_recv()
    tile_b[col] = jnp.sum(tile_a[...], axis=0)
    sums_col = []
    for step in range(1, N_COL):
        copy = pltpu.make_async_remote_copy(
            src_ref=tile_b.at[col], dst_ref=tile_b.at[col], send_sem=sum_send.at[7 + step], recv_sem=sum_recv.at[7 + step],
            device_id={"col": lax.rem(col + step, N_COL)}, device_id_type=MESH,
        )
        copy.start()
        sums_col.append(copy)
    arrive(fifth)
    for copy in sums_col:
        copy.wait_recv()
    moments = jnp.sum(tile_b[...], axis=0)
    m0, m1, m2, m3 = (moments[index : index + 1, 0:1] for index in range(4))

    step0 = m0 / (m0 + m1)
    rest = 1.0 - step0
    norm1 = rest * rest * m0 - 2.0 * step0 * rest * m1 + step0 * step0 * m2
    dir0, dir1 = rest + norm1 / m0, -step0
    curve = dir0 * dir0 * m0 + (dir0 * (dir0 + dir1) + dir0 * dir1) * m1 + (dir0 * dir1 + dir1 * (dir0 + dir1)) * m2 + dir1 * dir1 * m3
    step1 = norm1 / curve
    q0, q1, q2 = (ref[...].astype(F32) for ref in (rows0, rows1, rows2))
    inc = (step0 + step1 * dir0) * q0 + (step1 * dir1) * q1
    res = (rest - step1 * dir0) * q0 - (step0 + step1 * (dir0 + dir1)) * q1 - (step1 * dir1) * q2
    lift_low = lift[...].astype(BF)
    out_inc[...] = jnp.dot(inc.astype(BF), lift_low, preferred_element_type=F32).astype(BF)
    out_res[...] = jnp.dot(res.astype(BF), lift_low, preferred_element_type=F32).astype(BF)

    for copies in (col_copies, first, second, third, fourth, fifth, sums, sums_col):
        for copy in copies:
            copy.wait_send()


def expand(column_of, inc, res, out_inc, out_res):
    hit = jnp.where(column_of[:, 0:1] == iota((SLOTS, COLS_DEV), 1), 1.0, 0.0).astype(BF)
    contract = (((0,), (0,)), ((), ()))
    out_inc[0] = lax.dot_general(inc[...], hit, contract, preferred_element_type=F32)[0:LEV]
    out_res[0] = lax.dot_general(res[...], hit, contract, preferred_element_type=F32)[0:LEV]


def per_device(departures, obs_owner, obs_column, obs_count, channel_count, error_inv, jacobian, vertical):
    vmem, smem = pl.BlockSpec(memory_space=pltpu.VMEM), pl.BlockSpec(memory_space=pltpu.SMEM)
    hbm = pl.BlockSpec(memory_space=pl.ANY)
    dma = pltpu.SemaphoreType.DMA
    slab = pltpu.VMEM((SLOTS, FPAD), BF)
    wide = jax.ShapeDtypeStruct((SLOTS, NVAR * 256), BF)
    inc, res, column_of = pl.pallas_call(
        inner_loop,
        out_shape=(wide, wide, jax.ShapeDtypeStruct((SLOTS, 128), jnp.int32)),
        in_specs=[smem, smem, vmem, vmem, vmem, vmem, hbm, hbm],
        out_specs=(vmem, vmem, vmem),
        scratch_shapes=[
            pltpu.VMEM((NCHUNK, ROWS, CHUNK), F32),
            pltpu.VMEM((NCHUNK, FEAT, CHUNK), BF),
            pltpu.VMEM((FPAD, NVAR * 256), F32),
            pltpu.VMEM((FPAD, FPAD), F32),
            pltpu.VMEM((FPAD, FPAD), BF),
            pltpu.VMEM((FPAD, FPAD), F32),
            pltpu.VMEM((ROWS, FPAD), F32),
            *([slab] * 12),
            pltpu.VMEM((N_OBS, 8, 128), F32),
            pltpu.VMEM((N_COL, 8, 128), F32),
            dma((2, NCHUNK)),
            dma((N_COL,)),
            dma((N_COL,)),
            dma((5, N_OBS)),
            dma((5, N_OBS)),
            dma((24,)),
            dma((24,)),
        ],
        compiler_params=pltpu.CompilerParams(collective_id=0, has_side_effects=True, vmem_limit_bytes=40 << 20),
        name="inner_loop",
    )(
        obs_count, channel_count, obs_owner.reshape(1, ROWS), obs_column.reshape(1, ROWS), error_inv, vertical, departures, jacobian
    )
    out = jax.ShapeDtypeStruct((NVAR, LEV, COLS_DEV), F32)
    return pl.pallas_call(
        expand,
        grid=(NVAR,),
        out_shape=(out, out),
        in_specs=[
            pl.BlockSpec((SLOTS, 128), lambda var: (0, 0)),
            pl.BlockSpec((SLOTS, 256), lambda var: (0, var)),
            pl.BlockSpec((SLOTS, 256), lambda var: (0, var)),
        ],
        out_specs=(
            pl.BlockSpec((1, LEV, COLS_DEV), lambda var: (var, 0, 0)),
            pl.BlockSpec((1, LEV, COLS_DEV), lambda var: (var, 0, 0)),
        ),
        compiler_params=pltpu.CompilerParams(vmem_limit_bytes=32 << 20),
        name="expand",
    )(column_of, inc, res)


def solution(mesh):
    in_specs = (
        P(("col", "obs"), None),
        P(("col", "obs"), None),
        P(("col", "obs")),
        P(("col", "obs")),
        P("obs"),
        P("obs", None),
        P("obs", None, None),
        P(),
    )
    out_specs = (P(None, None, ("col", "obs")), P(None, None, ("col", "obs")))
    return jax.shard_map(per_device, mesh=mesh, in_specs=in_specs, out_specs=out_specs, check_vma=False)
```

time: 432 us -> 69.9 us (0.16); the launches traced: 425 us -> 69.5 us
  blocking collectives: 239 us -> 0 us
  Pallas kernels: 0 us -> 54.9 us
  local copies, waits for them, and re-layouts: 60.3 us -> 12.7 us
  matrix products: 43.3 us -> 0 us
  other arithmetic: 28.1 us -> 0 us
  starting transfers between devices: 25.6 us -> 0 us
  waiting for transfers between devices: 22.2 us -> 0 us
    psum x3 -> x0, blocking collectives: 188 us -> none  [the longest x2 125 us: squares(): return lax.psum(jnp.sum(field * field), ('col', 'obs'))]
    pallas_call x0 -> x2, Pallas kernels: none -> 54.9 us  [the longest x1 52.5 us: per_device(): pl.pallas_call(inner_loop, out_shape=(wide, wide, jax.ShapeDtypeStruct((S...]
    all_to_all x3 -> x0, blocking collectives: 50.8 us -> none  [the longest x2 33 us: backward(): lax.all_to_all(outgoing.astype(jnp.bfloat16), ('col', 'obs'), split_axis=...]
    dot_general x8 -> x0, matrix products: 43.3 us -> none  [the longest x3 17.4 us: adjoint_of(): lax.dot_general(weighted, jac_swath, contract, preferred_element_type=jnp...]
    all_to_all x3 -> x0, starting transfers between devices: 25.6 us -> none  [the longest x1 11.1 us: per_device(): lax.all_to_all(asked.reshape(device_count, capacity), ('col', 'obs'), spl...]
    all_to_all x3 -> x0, waiting for transfers between devices: 22.2 us -> none  [the longest x1 11.3 us: per_device(): lax.all_to_all(forward_outgoing, ('col', 'obs'), split_axis=0, concat_axi...]
    reshape x12 -> x0, local copies, waits for them, and re-layouts: 17 us -> none  [the longest x3 8.29 us: backward(): spread = summed.T.reshape(var_count, levels, columns_here)]
    convert_element_type x7 -> x0, local copies, waits for them, and re-layouts: 13 us -> none  [the longest x4 9.92 us: per_device(): packed = lifted.reshape(features, forward_columns_here).astype(jnp.bfloat16)]
  transfers between devices with their start and end apart: 3 -> 0, of which waited for: 3 -> 0; matrix products, arithmetic and copies ran while one was open for 2% -> 0% of each run, Pallas kernels for 0% -> 0%
where the time goes in v1:
time: 69.9 us; the launch traced here: 69.5 us
  Pallas kernels  54.9 us (79%)
  local copies, waits for them, and re-layouts  12.7 us (18%)
  between operations  1.95 us (3%)
    pallas_call x1, Pallas kernels, per_device(): pl.pallas_call(inner_loop, out_shape=(wide, wide, jax.ShapeDtypeStruct((S...  52.5 us
    unnamed x11, local copies, waits for them, and re-layouts  7.06 us
    pallas_call x2, local copies, waits for them, and re-layouts, per_device(): pl.pallas_call(expand, grid=(NVAR,), out_shape=(out, out), in_specs=[pl.B...  5.62 us
    pallas_call x1, Pallas kernels, per_device(): pl.pallas_call(expand, grid=(NVAR,), out_shape=(out, out), in_specs=[pl.B...  2.42 us

profile of v1, /device:TPU:0, one launch (start us, length us, event | category | flops | bytes accessed | tf_op | source)
XLA Modules:
  0.0 69.5 jit_solution(9503426480561644833)
XLA Ops:
  1.9 1.2 %copy.10.vertical = f32[4,137,137]{2,1,0:T(8,128)S(1)} copy(f32[4,137,137]{2,0,1:T(4,128)} %param.15) | data formatting | bytes 600608 | tf_op args[7]
  3.1 0.0 copy-start
  3.1 2.3 %copy-done = bf16[1,548,4096]{2,1,0:T(8,128)(2,1)S(1)} copy-done((bf16[1,548,4096]{2,1,0:T(8,128)(2,1)S(1)}, bf16[1,548,4096]{2,1,0:T(8,128)(2,1)}, u32[]{:S(2)}) %copy-start) | copy-done | bytes 4489240
  5.4 0.0 copy-start.1
  5.4 1.6 %copy-done.1 = f32[128,4096]{1,0:T(8,128)S(1)} copy-done((f32[128,4096]{1,0:T(8,128)S(1)}, f32[128,4096]{1,0:T(8,128)}, u32[]{:S(2)}) %copy-start.1) | copy-done | bytes 2097176
  7.0 0.0 copy-start.2
  7.0 0.7 %copy-done.2 = f32[1,4096]{1,0:T(1,128)S(1)} copy-done((f32[1,4096]{1,0:T(1,128)S(1)}, f32[1,4096]{1,0:T(1,128)}, u32[]{:S(2)}) %copy-start.2) | copy-done | bytes 16408
  7.7 0.0 copy-start.3
  7.7 0.7 copy-done.3
  8.3 0.0 copy-start.4
  8.3 0.7 copy-done.4
  9.0 52.5 %inner_loop.1 = (bf16[256,1024]{1,0:T(8,128)(2,1)S(1)}, bf16[256,1024]{1,0:T(8,128)(2,1)S(1)}, s32[256,128]{1,0:T(8,128)S(1)}) custom-call(s32[1]{0:T(128)S(6)} %copy.13.obs_count, s32[1]{0:T(128)S(6)} %copy.14.channel_count, s32[1,128]{1,0:T(1,128)S(1)} %bitcast.2, s32[1,128]{1,0:T(1,128)S(1)} %bitcast.3, f32[1,4096]{1,0:T(1,128)S(1)} %copy-done.2, ...), custom_call_target="tpu_custom_call" | custom-call | tf_op jit(solution)/shard_map/inner_loop/pallas_call | solution.py:258
  61.5 2.4 %expand.1 = (f32[4,137,1024]{2,1,0:T(8,128)S(1)}, f32[4,137,1024]{2,1,0:T(8,128)S(1)}) custom-call(s32[256,128]{1,0:T(8,128)S(1)} %get-tuple-element.5.column_of, bf16[256,1024]{1,0:T(8,128)(2,1)S(1)} %get-tuple-element.6.inc, bf16[256,1024]{1,0:T(8,128)(2,1)S(1)} %get-tuple-element.7.res), custom_call_target="tpu_custom_call" | custom-call | tf_op jit(solution)/shard_map/expand/pallas_call | solution.py:288
  63.9 2.8 %copy.11 = f32[4,137,1024]{2,0,1:T(4,128)} copy(f32[4,137,1024]{2,1,0:T(8,128)S(1)} %get-tuple-element.8) | data formatting | bytes 4489216 | tf_op jit(solution)/shard_map/expand/pallas_call | solution.py:288
  66.7 2.8 %copy.12 = f32[4,137,1024]{2,0,1:T(4,128)} copy(f32[4,137,1024]{2,1,0:T(8,128)S(1)} %get-tuple-element.9) | data formatting | bytes 4489216 | tf_op jit(solution)/shard_map/expand/pallas_call | solution.py:288
Async XLA Ops:
  3.1 2.3 %copy-start = (bf16[1,548,4096]{2,1,0:T(8,128)(2,1)S(1)}, bf16[1,548,4096]{2,1,0:T(8,128)(2,1)}, u32[]{:S(2)}) copy-start(bf16[1,548,4096]{2,1,0:T(8,128)(2,1)} %jac_hbm.1) | copy-start | bytes 13467652
  5.4 1.6 %copy-start.1 = (f32[128,4096]{1,0:T(8,128)S(1)}, f32[128,4096]{1,0:T(8,128)}, u32[]{:S(2)}) copy-start(f32[128,4096]{1,0:T(8,128)} %dep_hbm.1) | copy-start | bytes 6291460
  7.0 0.7 %copy-start.2 = (f32[1,4096]{1,0:T(1,128)S(1)}, f32[1,4096]{1,0:T(1,128)}, u32[]{:S(2)}) copy-start(f32[1,4096]{1,0:T(1,128)} %error_inv.1) | copy-start | bytes 49156
  7.7 0.7 copy-start.3
  8.3 0.7 copy-start.4

commit v2 on v1

v2 whole, which is shorter than its diff:
```python
import jax
import jax.numpy as jnp
from jax import lax
from jax.experimental import pallas as pl
from jax.experimental.pallas import tpu as pltpu
from jax.sharding import PartitionSpec as P

MESH = pl.DeviceIdType.MESH
BF = jnp.bfloat16
F32 = jnp.float32
COLS_DEV = 1024
NVAR, LEV = 4, 137
FEAT = NVAR * LEV
FPAD = 640
ROWS = 128
SLOTS = 256
CH = 4096
CHUNK = 1024
NCHUNK = CH // CHUNK
KERN_FIRST = 2
N_COL, N_OBS = 16, 8
COL_ROWS = SLOTS // N_COL
OBS_ROWS = SLOTS // N_OBS
NT = (((1,), (1,)), ((), ()))
N_CHIP = 4
CHIP_ROWS = 2 * OBS_ROWS
CHIP_ORDER = (2, 1, 3)
PLANE_ORDER = sorted(
    ((dx, dy) for dx in range(4) for dy in range(4) if dx or dy), key=lambda d: -(min(d[0], 4 - d[0]) + min(d[1], 4 - d[1]))
)


def iota(shape, axis):
    return lax.broadcasted_iota(jnp.int32, shape, axis)


def total(value):
    return jnp.sum(jnp.sum(value, axis=0, keepdims=True), axis=1, keepdims=True)


def inner_loop(
    count_hbm, channels_hbm, owner_hbm, column_hbm, error_hbm, vertical_hbm, dep_hbm, jac_hbm,
    out,
    obs_count, channel_count, owner, column, error_inv, vertical, dep, jac, lift, lift_low, gram, gram_low, kern, kacc, racc,
    same, full1, wide, split, sent, held, queued, rows0, prof0, hprof0, hadj0, rows1, prof1, hprof1, hadj1, rows2, tile_a, tile_b,
    in_sem, small_sem, col_send, col_recv, obs_send, obs_recv, sum_send, sum_recv,
):
    col, obs = lax.axis_index("col"), lax.axis_index("obs")
    chip, core = obs // 2, lax.rem(obs, 2)
    sibling = chip * 2 + 1 - core
    col_x, col_y = col // 4, lax.rem(col, 4)
    plane = [lax.rem(col_x + dx, 4) * 4 + lax.rem(col_y + dy, 4) for dx, dy in PLANE_ORDER]
    small = [
        pltpu.make_async_copy(source, target, small_sem.at[index])
        for index, (source, target) in enumerate((
            (vertical_hbm, vertical), (error_hbm, error_inv), (owner_hbm, owner), (column_hbm, column),
            (count_hbm, obs_count), (channels_hbm, channel_count),
        ))
    ]
    for copy in small:
        copy.start()

    def load(chunk):
        lanes = pl.ds(pl.multiple_of(chunk * CHUNK, CHUNK), CHUNK)
        return (
            pltpu.make_async_copy(jac_hbm.at[0, :, lanes], jac.at[chunk], in_sem.at[0, chunk]),
            pltpu.make_async_copy(dep_hbm.at[:, lanes], dep.at[chunk], in_sem.at[1, chunk]),
        )

    for chunk in range(NCHUNK):
        for copy in load(chunk):
            copy.start()

    barrier = pltpu.get_barrier_semaphore()
    for step in range(1, N_OBS):
        pl.semaphore_signal(barrier, inc=1, device_id={"obs": lax.rem(obs + step, N_OBS)}, device_id_type=MESH)
    for step in range(1, N_COL):
        pl.semaphore_signal(barrier, inc=1, device_id={"col": lax.rem(col + step, N_COL)}, device_id_type=MESH)

    for copy in small[1:]:
        copy.wait()

    owner_lanes = jnp.broadcast_to(owner[...].astype(F32), (ROWS, ROWS))
    owner_rows = owner_lanes.T
    earlier = jnp.where((owner_lanes == owner_rows) & (iota((ROWS, ROWS), 0) < iota((ROWS, ROWS), 1)), 1.0, 0.0)
    slot = owner[...] * 2 + jnp.sum(earlier, axis=0, keepdims=True).astype(jnp.int32)
    live_lanes = iota((1, ROWS), 1) < obs_count[0]
    place = jnp.where((iota((SLOTS, ROWS), 0) == slot) & live_lanes, 1.0, 0.0).astype(BF)
    column_rows = jnp.broadcast_to(column[...].astype(F32), (ROWS, ROWS)).T[:, 0:1]
    column_high = jnp.floor(column_rows * (1.0 / 32.0))
    column_low = column_rows - 32.0 * column_high

    def weights(chunk):
        lanes = pl.ds(pl.multiple_of(chunk * CHUNK, CHUNK), CHUNK)
        channel = chunk * CHUNK + iota((1, CHUNK), 1)
        return jnp.where(channel < channel_count[0], error_inv[:, lanes], 0.0)

    racc[...] = jnp.zeros_like(racc)

    def rhs_chunk(chunk, carry):
        for copy in load(chunk):
            copy.wait()
        weighted = (weights(chunk) * dep[chunk]).astype(BF)
        racc[:, 0:FEAT] += lax.dot_general(weighted, jac[chunk], NT, preferred_element_type=F32)
        return carry

    lax.fori_loop(0, NCHUNK, rhs_chunk, 0)
    lane = iota((ROWS, FPAD), 1)
    rows = racc[...]
    rows = jnp.where(lane == FEAT, column_high, rows)
    rows = jnp.where(lane == FEAT + 1, column_low, rows)
    rows = jnp.where(lane == FEAT + 2, 1.0, rows)
    sent[...] = jnp.dot(place, rows.astype(BF), preferred_element_type=F32).astype(BF)

    pl.semaphore_wait(barrier, N_OBS - 1 + N_COL - 1)

    def block(index, size):
        return pl.ds(pl.multiple_of(index * size, size), size)

    col_copies = []
    for step, other in enumerate(plane):
        copy = pltpu.make_async_remote_copy(
            src_ref=sent.at[block(other, COL_ROWS)], dst_ref=held.at[block(col, COL_ROWS)],
            send_sem=col_send.at[step], recv_sem=col_recv.at[step],
            device_id={"col": other}, device_id_type=MESH,
        )
        copy.start()
        col_copies.append(copy)
    held[block(col, COL_ROWS), :] = sent[block(col, COL_ROWS), :]

    lift[...] = jnp.zeros_like(lift)
    small[0].wait()
    for var in range(NVAR):
        lift[var * LEV : (var + 1) * LEV, var * 256 : var * 256 + LEV] = vertical[:, var, :]
    gram[...] = jnp.zeros_like(gram)
    for var in range(NVAR):
        part = lift[var * 128 : var * 128 + 256, var * 256 : var * 256 + 256]
        square = lax.dot_general(part, part, NT, precision=lax.Precision.HIGHEST, preferred_element_type=F32)
        where = slice(var * 128, var * 128 + 256)
        gram[where, where] = gram[where, where] + square

    gram_low[...] = gram[...].astype(BF)
    kacc[...] = jnp.zeros_like(kacc)

    def kern_chunk(chunk, carry):
        block_in = jac[chunk]
        scaled = (block_in.astype(F32) * weights(chunk)).astype(BF)
        kacc[0:FEAT, 0:FEAT] += lax.dot_general(scaled, block_in, NT, preferred_element_type=F32)
        return carry

    lax.fori_loop(0, KERN_FIRST, kern_chunk, 0)

    for copy in col_copies:
        copy.wait_recv()

    target, source = iota((SLOTS, SLOTS), 0), iota((SLOTS, SLOTS), 1)
    wanted = lax.rem(target // 2, N_COL) * COL_ROWS + (target // OBS_ROWS) * 2 + lax.rem(target, 2)
    turn = jnp.where(source == wanted, 1.0, 0.0).astype(BF)
    queued[...] = jnp.dot(turn, held[...], preferred_element_type=F32).astype(BF)

    sends = []

    def rows_to(number, away, source_ref, target_ref):
        there = lax.rem(chip + away, N_CHIP)
        if away == 0:
            target_ref[block(obs, OBS_ROWS), :] = source_ref[block(obs, OBS_ROWS), :]
            others = ((1, sibling),)
        else:
            others = ((0, there * 2 + core), (1, there * 2 + 1 - core))
        for which, other in others:
            copy = pltpu.make_async_remote_copy(
                src_ref=source_ref.at[block(other, OBS_ROWS)], dst_ref=target_ref.at[block(obs, OBS_ROWS)],
                send_sem=obs_send.at[number, 2 * away + which], recv_sem=obs_recv.at[number, 2 * away + which],
                device_id={"obs": other}, device_id_type=MESH,
            )
            copy.start()
            sends.append(copy)

    def rows_from(number, away, target_ref):
        there = lax.rem(chip + N_CHIP - away, N_CHIP)
        others = ((1, sibling),) if away == 0 else ((0, there * 2 + core), (1, there * 2 + 1 - core))
        for which, other in others:
            pltpu.make_async_remote_copy(
                src_ref=target_ref.at[block(other, OBS_ROWS)], dst_ref=target_ref.at[block(other, OBS_ROWS)],
                send_sem=obs_send.at[number, 2 * away + which], recv_sem=obs_recv.at[number, 2 * away + which],
                device_id={"obs": other}, device_id_type=MESH,
            ).wait_recv()
        return block(there, CHIP_ROWS)

    for away in (*CHIP_ORDER, 0):
        rows_to(0, away, queued, rows0)
    lax.fori_loop(KERN_FIRST, NCHUNK, kern_chunk, 0)
    diagonal = iota((FPAD, FPAD), 0) == iota((FPAD, FPAD), 1)
    diagonal = diagonal & (iota((FPAD, FPAD), 0) < FEAT)
    shift = (total(jnp.where(diagonal, kacc[...], 0.0)) * (1.0 / FEAT)).astype(BF).astype(F32)
    kern[...] = jnp.where(diagonal, kacc[...] - shift, kacc[...]).astype(BF)

    lane_of = iota((256, FPAD), 1)
    for var in range(NVAR):
        turned = jnp.where(lane_of == iota((256, FPAD), 0) * NVAR + var, 1.0, 0.0).astype(BF)
        part = lift[var * 128 : var * 128 + 256, var * 256 : var * 256 + 256].astype(BF)
        placed = jnp.dot(part, turned, preferred_element_type=F32).astype(BF)
        if var == 0:
            lift_low[0:256] = placed
        else:
            lift_low[var * 128 : var * 128 + 128] += placed[0:128]
            lift_low[var * 128 + 128 : var * 128 + 256] = placed[128:256]

    for away in (0, *CHIP_ORDER):
        rows_from(0, away, rows0)

    extra = rows0[:, 512:640].astype(F32)
    extra_lanes = extra.T
    at = FEAT - 512
    live = extra[:, at + 2 : at + 3]
    column_of = jnp.where(live > 0.5, extra[:, at : at + 1] * 32.0 + extra[:, at + 1 : at + 2], -1.0)
    column_across = jnp.where(
        extra_lanes[at + 2 : at + 3, :] > 0.5,
        extra_lanes[at : at + 1, :] * 32.0 + extra_lanes[at + 1 : at + 2, :],
        -2.0,
    )
    same[...] = jnp.where(column_of == column_across, 1.0, 0.0).astype(BF)

    def halves(value):
        high = value.astype(BF)
        return high, (value - high.astype(F32)).astype(BF)

    def send_profiles(number, gathered, prof_ref, target_ref, own):
        high, low = halves(gathered)
        split[0] = high
        split[1] = low
        moment = jnp.zeros((1, 1), F32)
        for away in (*CHIP_ORDER, 0):
            here = block(lax.rem(chip + away, N_CHIP), CHIP_ROWS)
            pair = jnp.concatenate([split[0, here, :], split[1, here, :]], axis=0)
            both = jnp.dot(pair, gram_low[...], preferred_element_type=F32)
            lifted = both[0:CHIP_ROWS] + both[CHIP_ROWS:]
            prof_ref[here, :] = lifted.astype(BF)
            rows_to(number, away, prof_ref, target_ref)
            moment += total(lifted * own[here, :].astype(F32))
        return moment

    def apply_kern(number, prof_ref, adj_ref, target_ref, after):
        moment = jnp.zeros((1, 1), F32)
        lane_here = iota((CHIP_ROWS, FPAD), 1)
        for away in (0, 1, 3, 2):
            here = rows_from(number, away, prof_ref)
            profiles = prof_ref[here, :]
            adjoint = jnp.dot(profiles, kern[...], preferred_element_type=F32)
            adj_ref[here, :] = jnp.where(lane_here == FEAT, shift, adjoint).astype(BF)
            profiles = profiles.astype(F32)
            if after is None:
                rows_to(number + 1, (N_CHIP - away) % N_CHIP, adj_ref, target_ref)
            moment += total(profiles * (adjoint + shift * profiles))
            if after is not None:
                if away == 2:
                    after(moment)
                rows_to(number + 1, (N_CHIP - away) % N_CHIP, adj_ref, target_ref)
        return moment

    def whole(adj_ref, prof_ref):
        adjoint = adj_ref[...].astype(F32)
        shifts = adjoint[:, FEAT : FEAT + 1]
        return jnp.where(iota((SLOTS, FPAD), 1) < FEAT, adjoint + shifts * prof_ref[...].astype(F32), 0.0)

    gathered = jnp.dot(same[...], rows0[...], preferred_element_type=F32)
    moment0 = send_profiles(1, gathered, prof0, hprof0, rows0)
    moment1 = apply_kern(1, hprof0, hadj0, rows1, None)
    for away in (0, *CHIP_ORDER):
        rows_from(2, away, rows1)
    full1[...] = whole(rows1, prof0)
    high, low = halves(full1[...])
    gathered = jnp.dot(same[...], high, preferred_element_type=F32) + jnp.dot(same[...], low, preferred_element_type=F32)
    moment2 = send_profiles(3, gathered, prof1, hprof1, full1)

    row = iota((8, 128), 0)
    sums = []

    def send_moments(moment3):
        tile_a[obs] = jnp.where(
            row == 0, moment0, jnp.where(row == 1, moment1, jnp.where(row == 2, moment2, jnp.where(row == 3, moment3, 0.0)))
        )
        for step in (4, 5, 3, 2, 6, 7, 1):
            copy = pltpu.make_async_remote_copy(
                src_ref=tile_a.at[obs], dst_ref=tile_a.at[obs], send_sem=sum_send.at[step], recv_sem=sum_recv.at[step],
                device_id={"obs": lax.rem(obs + step, N_OBS)}, device_id_type=MESH,
            )
            copy.start()
            sums.append(copy)

    apply_kern(3, hprof1, hadj1, rows2, send_moments)
    for copy in sums:
        copy.wait_recv()
    tile_b[col] = jnp.sum(tile_a[...], axis=0)
    sums_col = []
    for step, other in enumerate(plane):
        copy = pltpu.make_async_remote_copy(
            src_ref=tile_b.at[col], dst_ref=tile_b.at[col], send_sem=sum_send.at[8 + step], recv_sem=sum_recv.at[8 + step],
            device_id={"col": other}, device_id_type=MESH,
        )
        copy.start()
        sums_col.append(copy)
    for away in (0, *CHIP_ORDER):
        rows_from(4, away, rows2)
    wide[0] = jnp.dot(rows0[...], lift_low[...], preferred_element_type=F32)
    high, low = halves(full1[...])
    wide[1] = jnp.dot(high, lift_low[...], preferred_element_type=F32) + jnp.dot(low, lift_low[...], preferred_element_type=F32)
    high, low = halves(whole(rows2, prof1))
    wide[2] = jnp.dot(high, lift_low[...], preferred_element_type=F32) + jnp.dot(low, lift_low[...], preferred_element_type=F32)
    for copy in sums_col:
        copy.wait_recv()
    moments = jnp.sum(tile_b[...], axis=0)
    m0, m1, m2, m3 = (moments[index : index + 1, 0:1] for index in range(4))

    step0 = m0 / (m0 + m1)
    rest = 1.0 - step0
    norm1 = rest * rest * m0 - 2.0 * step0 * rest * m1 + step0 * step0 * m2
    dir0, dir1 = rest + norm1 / m0, -step0
    curve = dir0 * dir0 * m0 + (dir0 * (dir0 + dir1) + dir0 * dir1) * m1 + (dir0 * dir1 + dir1 * (dir0 + dir1)) * m2 + dir1 * dir1 * m3
    step1 = norm1 / curve
    tail = iota((SLOTS, FPAD), 1) >= FEAT
    inc = (step0 + step1 * dir0) * wide[0] + (step1 * dir1) * wide[1]
    res = (rest - step1 * dir0) * wide[0] - (step0 + step1 * (dir0 + dir1)) * wide[1] - (step1 * dir1) * wide[2]
    out[0] = jnp.where(tail, rows0[...].astype(F32), inc).astype(BF)
    out[1] = jnp.where(tail, 0.0, res).astype(BF)

    for copy in (*col_copies, *sends, *sums, *sums_col):
        copy.wait_send()


def expand(packed, out_inc, out_res, taken, full_inc, full_res, in_sem, out_sem):
    parts = FPAD // 128
    levels = 128 // NVAR
    order = (parts - 1, *range(parts - 1))
    loads = [
        pltpu.make_async_copy(packed.at[:, :, pl.ds(128 * part, 128)], taken.at[part], in_sem.at[part]) for part in range(parts)
    ]
    for part in order:
        loads[part].start()
    loads[parts - 1].wait()
    extra = taken[parts - 1, 0].astype(F32)
    at = FEAT - 512
    column_of = jnp.where(extra[:, at + 2 : at + 3] > 0.5, extra[:, at : at + 1] * 32.0 + extra[:, at + 1 : at + 2], -1.0)
    hit = jnp.where(column_of.astype(jnp.int32) == iota((SLOTS, COLS_DEV), 1), 1.0, 0.0).astype(BF)
    contract = (((0,), (0,)), ((), ()))
    stores = []
    for part in order:
        if part < parts - 1:
            loads[part].wait()
        count = min(levels, LEV - levels * part)
        for index, (full, out) in enumerate(((full_inc, out_inc), (full_res, out_res))):
            values = lax.dot_general(taken[part, index], hit, contract, preferred_element_type=F32)
            full[levels * part : levels * part + count] = values[0 : NVAR * count].reshape(count, NVAR, COLS_DEV)
            here = pl.ds(levels * part, count)
            store = pltpu.make_async_copy(full.at[here], out.at[here], out_sem.at[part, index])
            store.start()
            stores.append(store)
    for store in stores:
        store.wait()


def per_device(departures, obs_owner, obs_column, obs_count, channel_count, error_inv, jacobian, vertical):
    vmem, hbm = pl.BlockSpec(memory_space=pltpu.VMEM), pl.BlockSpec(memory_space=pltpu.HBM)
    dma = pltpu.SemaphoreType.DMA
    slab = pltpu.VMEM((SLOTS, FPAD), BF)
    packed = pl.pallas_call(
        inner_loop,
        out_shape=jax.ShapeDtypeStruct((2, SLOTS, FPAD), BF),
        in_specs=[hbm] * 8,
        out_specs=vmem,
        scratch_shapes=[
            pltpu.SMEM((1,), jnp.int32),
            pltpu.SMEM((1,), jnp.int32),
            pltpu.VMEM((1, ROWS), jnp.int32),
            pltpu.VMEM((1, ROWS), jnp.int32),
            pltpu.VMEM((1, CH), F32),
            pltpu.VMEM((LEV, NVAR, LEV), F32),
            pltpu.VMEM((NCHUNK, ROWS, CHUNK), F32),
            pltpu.VMEM((NCHUNK, FEAT, CHUNK), BF),
            pltpu.VMEM((FPAD, NVAR * 256), F32),
            pltpu.VMEM((FPAD, FPAD), BF),
            pltpu.VMEM((FPAD, FPAD), F32),
            pltpu.VMEM((FPAD, FPAD), BF),
            pltpu.VMEM((FPAD, FPAD), BF),
            pltpu.VMEM((FPAD, FPAD), F32),
            pltpu.VMEM((ROWS, FPAD), F32),
            pltpu.VMEM((SLOTS, SLOTS), BF),
            pltpu.VMEM((SLOTS, FPAD), F32),
            pltpu.VMEM((3, SLOTS, FPAD), F32),
            pltpu.VMEM((2, SLOTS, FPAD), BF),
            *([slab] * 12),
            pltpu.VMEM((N_OBS, 8, 128), F32),
            pltpu.VMEM((N_COL, 8, 128), F32),
            dma((2, NCHUNK)),
            dma((6,)),
            dma((N_COL,)),
            dma((N_COL,)),
            dma((5, N_OBS)),
            dma((5, N_OBS)),
            dma((24,)),
            dma((24,)),
        ],
        compiler_params=pltpu.CompilerParams(collective_id=0, has_side_effects=True, vmem_limit_bytes=62 << 20),
        name="inner_loop",
    )(
        obs_count, channel_count, obs_owner.reshape(1, ROWS), obs_column.reshape(1, ROWS), error_inv,
        vertical.transpose(1, 0, 2), departures, jacobian,
    )
    out = jax.ShapeDtypeStruct((LEV, NVAR, COLS_DEV), F32)
    inc, res = pl.pallas_call(
        expand,
        out_shape=(out, out),
        in_specs=[hbm],
        out_specs=(hbm, hbm),
        scratch_shapes=[
            pltpu.VMEM((FPAD // 128, 2, SLOTS, 128), BF),
            pltpu.VMEM((LEV, NVAR, COLS_DEV), F32),
            pltpu.VMEM((LEV, NVAR, COLS_DEV), F32),
            dma((FPAD // 128,)),
            dma((FPAD // 128, 2)),
        ],
        compiler_params=pltpu.CompilerParams(vmem_limit_bytes=62 << 20),
        name="expand",
    )(packed)
    return inc.transpose(1, 0, 2), res.transpose(1, 0, 2)


def solution(mesh):
    in_specs = (
        P(("col", "obs"), None),
        P(("col", "obs"), None),
        P(("col", "obs")),
        P(("col", "obs")),
        P("obs"),
        P("obs", None),
        P("obs", None, None),
        P(),
    )
    out_specs = (P(None, None, ("col", "obs")), P(None, None, ("col", "obs")))
    return jax.shard_map(per_device, mesh=mesh, in_specs=in_specs, out_specs=out_specs, check_vma=False)
```

time: 69.9 us -> 59.1 us (0.85)
  local copies, waits for them, and re-layouts: 12.7 us -> 0 us
  Pallas kernels: 54.9 us -> 56.6 us
    unnamed x11 -> x0, local copies, waits for them, and re-layouts: 7.06 us -> none
    pallas_call x2 -> x0, local copies, waits for them, and re-layouts: 5.62 us -> none  [per_device(): pl.pallas_call(expand, grid=(NVAR,), out_shape=(out, out), in_specs=[pl.B...]
    pallas_call x2, Pallas kernels: 54.9 us -> 56.6 us  [the longest x1 52.7 us: per_device(): pl.pallas_call(inner_loop, out_shape=jax.ShapeDtypeStruct((2, SLOTS, FPAD...]
where the time goes in v2:
time: 59.1 us; the launch traced here: 58.7 us
  Pallas kernels  56.6 us (96%)
  between operations  2.09 us (4%)
    pallas_call x1, Pallas kernels, per_device(): pl.pallas_call(inner_loop, out_shape=jax.ShapeDtypeStruct((2, SLOTS, FPAD...  52.7 us
    pallas_call x1, Pallas kernels, per_device(): pl.pallas_call(expand, out_shape=(out, out), in_specs=[hbm], out_specs=(h...  3.85 us

profile of v2, /device:TPU:0, one launch (start us, length us, event | category | flops | bytes accessed | tf_op | source)
XLA Modules:
  0.0 58.7 jit_solution(83874235564792442)
XLA Ops:
  1.9 52.7 %inner_loop.1.packed = bf16[2,256,640]{2,1,0:T(8,128)(2,1)} custom-call(s32[1]{0:T(128)S(6)} %copy.10.count_hbm, s32[1]{0:T(128)S(6)} %copy.11.channels_hbm, s32[1,128]{1,0:T(1,128)} %bitcast.6, s32[1,128]{1,0:T(1,128)} %bitcast.7, f32[1,4096]{1,0:T(1,128)} %error_hbm.1, f32[137,4,137]{2,1,0:T(4,128)} %bitcast.5, f32[128,4096]{1,0:T(8,128)} %dep_hbm.1, ...), custom_call_target="tpu_custom_call" | custom-call | tf_op jit(solution)/shard_map/inner_loop/pallas_call | solution.py:366
  54.7 3.8 %expand.1 = (f32[137,4,1024]{2,1,0:T(4,128)}, f32[137,4,1024]{2,1,0:T(4,128)}) custom-call(bf16[2,256,640]{2,1,0:T(8,128)(2,1)} %inner_loop.1.packed), custom_call_target="tpu_custom_call" | custom-call | tf_op jit(solution)/shard_map/expand/pallas_call | solution.py:410

commit v3 on v2

--- a/solution.py
+++ b/solution.py
@@ -17,7 +17,10 @@
 CH = 4096
 CHUNK = 1024
 NCHUNK = CH // CHUNK
-KERN_FIRST = 2
+K_PARTS = ((0, 560, 0), (128, 432, 128), (640, 304, 0), (768, 176, 128), (1024, 48, 0))
+K_FREE = ((560, 80), (944, 80), (1072, 80))
+K_ROWS = 1152
+GUESTS = 5
 N_COL, N_OBS = 16, 8
 COL_ROWS = SLOTS // N_COL
 OBS_ROWS = SLOTS // N_OBS
@@ -42,8 +45,8 @@
     count_hbm, channels_hbm, owner_hbm, column_hbm, error_hbm, vertical_hbm, dep_hbm, jac_hbm,
     out,
     obs_count, channel_count, owner, column, error_inv, vertical, dep, jac, lift, lift_low, gram, gram_low, kern, kacc, racc,
-    same, full1, wide, split, sent, held, queued, rows0, prof0, hprof0, hadj0, rows1, prof1, hprof1, hadj1, rows2, tile_a, tile_b,
-    in_sem, small_sem, col_send, col_recv, obs_send, obs_recv, sum_send, sum_recv,
+    same, full1, wide, split, sent, held, queued, rows0, prof0, rows1, prof1, rows2, guest0, reply0, guest1, reply1, tile_a, tile_b,
+    in_sem, small_sem, col_send, col_recv, obs_send, obs_recv, kern_send, kern_recv, leg_send, leg_recv, sum_send, sum_recv,
 ):
     col, obs = lax.axis_index("col"), lax.axis_index("obs")
     chip, core = obs // 2, lax.rem(obs, 2)
@@ -128,27 +131,54 @@
         col_copies.append(copy)
     held[block(col, COL_ROWS), :] = sent[block(col, COL_ROWS), :]
 
-    lift[...] = jnp.zeros_like(lift)
-    small[0].wait()
-    for var in range(NVAR):
-        lift[var * LEV : (var + 1) * LEV, var * 256 : var * 256 + LEV] = vertical[:, var, :]
-    gram[...] = jnp.zeros_like(gram)
-    for var in range(NVAR):
-        part = lift[var * 128 : var * 128 + 256, var * 256 : var * 256 + 256]
-        square = lax.dot_general(part, part, NT, precision=lax.Precision.HIGHEST, preferred_element_type=F32)
-        where = slice(var * 128, var * 128 + 256)
-        gram[where, where] = gram[where, where] + square
-
-    gram_low[...] = gram[...].astype(BF)
-    kacc[...] = jnp.zeros_like(kacc)
-
-    def kern_chunk(chunk, carry):
-        block_in = jac[chunk]
-        scaled = (block_in.astype(F32) * weights(chunk)).astype(BF)
-        kacc[0:FEAT, 0:FEAT] += lax.dot_general(scaled, block_in, NT, preferred_element_type=F32)
-        return carry
-
-    lax.fori_loop(0, KERN_FIRST, kern_chunk, 0)
+    for first, count in K_FREE:
+        kern[:, first : first + count, :] = jnp.zeros((3, count, 256), BF)
+    kern_copies = []
+    diagonal = iota((128, 128), 0) == iota((128, 128), 1)
+
+    def kern_part(which, index):
+        first, count, lane_at = K_PARTS[index]
+        return kern.at[which, pl.ds(first, count), pl.ds(lane_at, 128)]
+
+    def make_kern(index, shift):
+        first, count, lane_at = K_PARTS[index]
+        lanes = slice(lane_at, lane_at + 128)
+        top = index * 128
+        wide_rows = min(128, FEAT - top)
+        kacc[...] = jnp.zeros_like(kacc)
+
+        def kern_chunk(chunk, carry):
+            scaled = (jac[chunk, top : top + wide_rows, :].astype(F32) * weights(chunk)).astype(BF)
+            kacc[0 : FEAT - top, 0:wide_rows] += lax.dot_general(
+                jac[chunk, top:FEAT, :], scaled, NT, preferred_element_type=F32
+            )
+            return carry
+
+        lax.fori_loop(0, NCHUNK, kern_chunk, 0)
+        if index == 0:
+            shift = (total(jnp.where(diagonal, kacc[0:128], 0.0)) * (1.0 / 128)).astype(BF).astype(F32)
+        if wide_rows < 128:
+            corner = jnp.where(diagonal, kacc[0:128] - shift, kacc[0:128])
+            kern[1, first : first + count, lanes] = jnp.where(iota((128, 128), 0) < wide_rows, corner, shift)[0:count].astype(BF)
+        else:
+            kern[1, first : first + 128, lanes] = jnp.where(diagonal, kacc[0:128] - shift, kacc[0:128]).astype(BF)
+            kern[1, first + 128 : first + count, lanes] = kacc[128:count].astype(BF)
+        for target, away in ((0, 1), (2, 3)):
+            copy = pltpu.make_async_remote_copy(
+                src_ref=kern_part(1, index), dst_ref=kern_part(target, index),
+                send_sem=kern_send.at[target, index], recv_sem=kern_recv.at[target, index],
+                device_id={"obs": lax.rem(chip + away, N_CHIP) * 2 + core}, device_id_type=MESH,
+            )
+            copy.start()
+            kern_copies.append(copy)
+        return shift
+
+    def fill_kern(which):
+        for first in (0, 640):
+            kern[which, first : first + 128, 128:256] = kern[which, first + 128 : first + 256, 0:128].astype(F32).T.astype(BF)
+
+    shift = make_kern(0, None)
+    make_kern(1, shift)
 
     for copy in col_copies:
         copy.wait_recv()
@@ -189,12 +219,21 @@
 
     for away in (*CHIP_ORDER, 0):
         rows_to(0, away, queued, rows0)
-    lax.fori_loop(KERN_FIRST, NCHUNK, kern_chunk, 0)
-    diagonal = iota((FPAD, FPAD), 0) == iota((FPAD, FPAD), 1)
-    diagonal = diagonal & (iota((FPAD, FPAD), 0) < FEAT)
-    shift = (total(jnp.where(diagonal, kacc[...], 0.0)) * (1.0 / FEAT)).astype(BF).astype(F32)
-    kern[...] = jnp.where(diagonal, kacc[...] - shift, kacc[...]).astype(BF)
-
+    for index in (2, 3, 4):
+        make_kern(index, shift)
+    fill_kern(1)
+    lift[...] = jnp.zeros_like(lift)
+    small[0].wait()
+    for var in range(NVAR):
+        lift[var * LEV : (var + 1) * LEV, var * 256 : var * 256 + LEV] = vertical[:, var, :]
+    gram[...] = jnp.zeros_like(gram)
+    for var in range(NVAR):
+        part = lift[var * 128 : var * 128 + 256, var * 256 : var * 256 + 256]
+        square = lax.dot_general(part, part, NT, precision=lax.Precision.HIGHEST, preferred_element_type=F32)
+        where = slice(var * 128, var * 128 + 256)
+        gram[where, where] = gram[where, where] + square
+
+    gram_low[...] = gram[...].astype(BF)
     lane_of = iota((256, FPAD), 1)
     for var in range(NVAR):
         turned = jnp.where(lane_of == iota((256, FPAD), 0) * NVAR + var, 1.0, 0.0).astype(BF)
@@ -236,27 +275,84 @@
             both = jnp.dot(pair, gram_low[...], preferred_element_type=F32)
             lifted = both[0:CHIP_ROWS] + both[CHIP_ROWS:]
             prof_ref[here, :] = lifted.astype(BF)
-            rows_to(number, away, prof_ref, target_ref)
+            profiles_to(number, away, prof_ref, target_ref)
             moment += total(lifted * own[here, :].astype(F32))
         return moment
 
-    def apply_kern(number, prof_ref, adj_ref, target_ref, after):
+    def slab(chip_index, core_index):
+        return block(lax.rem(chip_index, N_CHIP) * 2 + core_index, OBS_ROWS)
+
+    def copy_of(number, source, target, send, recv, device):
+        return pltpu.make_async_remote_copy(
+            src_ref=source, dst_ref=target, send_sem=leg_send.at[number, send], recv_sem=leg_recv.at[number, recv],
+            device_id={"obs": device}, device_id_type=MESH,
+        )
+
+    helper = lax.rem(chip + 1 + 2 * core, N_CHIP)
+
+    def go(copy):
+        copy.start()
+        sends.append(copy)
+
+    def profiles_to(number, away, prof_ref, guest_ref):
+        if away == 2:
+            for other in range(2):
+                go(copy_of(number, prof_ref.at[slab(chip + 2, other)], guest_ref.at[4 - core], 3 + other, 4 - core, helper * 2 + other))
+        else:
+            slot = (away + 1) % N_CHIP
+            go(copy_of(number, prof_ref.at[slab(chip + away, 1 - core)], guest_ref.at[slot], slot, slot, sibling))
+
+    def apply_kern(number, prof_ref, guest_ref, reply_ref, target_ref, after):
         moment = jnp.zeros((1, 1), F32)
-        lane_here = iota((CHIP_ROWS, FPAD), 1)
-        for away in (0, 1, 3, 2):
-            here = rows_from(number, away, prof_ref)
-            profiles = prof_ref[here, :]
-            adjoint = jnp.dot(profiles, kern[...], preferred_element_type=F32)
-            adj_ref[here, :] = jnp.where(lane_here == FEAT, shift, adjoint).astype(BF)
+        for which, guests in ((1, (1,)), (0, (3, 0)), (2, (4, 2))):
+            own = slab(chip + which + 3, core)
+            for guest in guests:
+                copy_of(number, guest_ref.at[guest], guest_ref.at[guest], guest, guest, sibling).wait_recv()
+            if number == 0 and which != 1:
+                for index in range(len(K_PARTS)):
+                    part = kern_part(which, index)
+                    pltpu.make_async_remote_copy(
+                        src_ref=part, dst_ref=part, send_sem=kern_send.at[which, index], recv_sem=kern_recv.at[which, index],
+                        device_id={"obs": sibling}, device_id_type=MESH,
+                    ).wait_recv()
+                fill_kern(which)
+            profiles = jnp.concatenate([prof_ref[own, :]] + [guest_ref[guest] for guest in guests], axis=0)
+            left, middle, right = profiles[:, 0:256], profiles[:, 256:512], profiles[:, 512:640]
+            dot = lambda one, two: jnp.dot(one, two, preferred_element_type=F32)
+            dot_turned = lambda one, two: lax.dot_general(one, two, NT, preferred_element_type=F32)
+            adjoint = jnp.concatenate(
+                [
+                    dot(profiles, kern[which, 0:640, :]),
+                    dot_turned(left, kern[which, 256:512, :]) + dot(profiles[:, 256:640], kern[which, 640:1024, :]),
+                    dot_turned(left, kern[which, 512:640, :]) + dot_turned(middle, kern[which, 896:1024, :])
+                    + dot(right, kern[which, 1024:1152, 0:128]),
+                ],
+                axis=1,
+            )
+            away_shift = kern[which, 1056:1072, 0:128].astype(F32)[8:9, 0:1]
+            rows_out = jnp.where(iota(adjoint.shape, 1) == FEAT, away_shift, adjoint).astype(BF)
             profiles = profiles.astype(F32)
-            if after is None:
-                rows_to(number + 1, (N_CHIP - away) % N_CHIP, adj_ref, target_ref)
-            moment += total(profiles * (adjoint + shift * profiles))
-            if after is not None:
-                if away == 2:
-                    after(moment)
-                rows_to(number + 1, (N_CHIP - away) % N_CHIP, adj_ref, target_ref)
+            moment += total(profiles * (adjoint + away_shift * profiles))
+            target_ref[own, :] = rows_out[0:OBS_ROWS]
+            for index, guest in enumerate(guests):
+                reply_ref[guest] = rows_out[(index + 1) * OBS_ROWS : (index + 2) * OBS_ROWS]
+            if after is not None and which == 2:
+                after(moment)
+            for guest in guests:
+                if guest < 3:
+                    go(copy_of(number + 1, reply_ref.at[guest], target_ref.at[own], guest, guest, sibling))
+                else:
+                    back = lax.rem(chip + (1 if guest == 3 else 3), N_CHIP) * 2 + (1 if guest == 3 else 0)
+                    go(copy_of(number + 1, reply_ref.at[guest], target_ref.at[own], guest, 3 + core, back))
         return moment
+
+    def replies(number, target_ref):
+        for slot in range(3):
+            here = target_ref.at[slab(chip + slot + 3, 1 - core)]
+            copy_of(number, here, here, slot, slot, sibling).wait_recv()
+        for other in range(2):
+            here = target_ref.at[slab(chip + 2, other)]
+            copy_of(number, here, here, 3 + other, 3 + other, sibling).wait_recv()
 
     def whole(adj_ref, prof_ref):
         adjoint = adj_ref[...].astype(F32)
@@ -264,14 +360,13 @@
         return jnp.where(iota((SLOTS, FPAD), 1) < FEAT, adjoint + shifts * prof_ref[...].astype(F32), 0.0)
 
     gathered = jnp.dot(same[...], rows0[...], preferred_element_type=F32)
-    moment0 = send_profiles(1, gathered, prof0, hprof0, rows0)
-    moment1 = apply_kern(1, hprof0, hadj0, rows1, None)
-    for away in (0, *CHIP_ORDER):
-        rows_from(2, away, rows1)
+    moment0 = send_profiles(0, gathered, prof0, guest0, rows0)
+    moment1 = apply_kern(0, prof0, guest0, reply0, rows1, None)
+    replies(1, rows1)
     full1[...] = whole(rows1, prof0)
     high, low = halves(full1[...])
     gathered = jnp.dot(same[...], high, preferred_element_type=F32) + jnp.dot(same[...], low, preferred_element_type=F32)
-    moment2 = send_profiles(3, gathered, prof1, hprof1, full1)
+    moment2 = send_profiles(2, gathered, prof1, guest1, full1)
 
     row = iota((8, 128), 0)
     sums = []
@@ -288,7 +383,7 @@
             copy.start()
             sums.append(copy)
 
-    apply_kern(3, hprof1, hadj1, rows2, send_moments)
+    apply_kern(2, prof1, guest1, reply1, rows2, send_moments)
     for copy in sums:
         copy.wait_recv()
     tile_b[col] = jnp.sum(tile_a[...], axis=0)
@@ -300,8 +395,7 @@
         )
         copy.start()
         sums_col.append(copy)
-    for away in (0, *CHIP_ORDER):
-        rows_from(4, away, rows2)
+    replies(3, rows2)
     wide[0] = jnp.dot(rows0[...], lift_low[...], preferred_element_type=F32)
     high, low = halves(full1[...])
     wide[1] = jnp.dot(high, lift_low[...], preferred_element_type=F32) + jnp.dot(low, lift_low[...], preferred_element_type=F32)
@@ -324,7 +418,7 @@
     out[0] = jnp.where(tail, rows0[...].astype(F32), inc).astype(BF)
     out[1] = jnp.where(tail, 0.0, res).astype(BF)
 
-    for copy in (*col_copies, *sends, *sums, *sums_col):
+    for copy in (*col_copies, *kern_copies, *sends, *sums, *sums_col):
         copy.wait_send()
 
 
@@ -381,22 +475,27 @@
             pltpu.VMEM((FPAD, FPAD), BF),
             pltpu.VMEM((FPAD, FPAD), F32),
             pltpu.VMEM((FPAD, FPAD), BF),
-            pltpu.VMEM((FPAD, FPAD), BF),
-            pltpu.VMEM((FPAD, FPAD), F32),
+            pltpu.VMEM((3, K_ROWS, 256), BF),
+            pltpu.VMEM((FPAD, 128), F32),
             pltpu.VMEM((ROWS, FPAD), F32),
             pltpu.VMEM((SLOTS, SLOTS), BF),
             pltpu.VMEM((SLOTS, FPAD), F32),
             pltpu.VMEM((3, SLOTS, FPAD), F32),
             pltpu.VMEM((2, SLOTS, FPAD), BF),
-            *([slab] * 12),
+            *([slab] * 8),
+            *([pltpu.VMEM((GUESTS, OBS_ROWS, FPAD), BF)] * 4),
             pltpu.VMEM((N_OBS, 8, 128), F32),
             pltpu.VMEM((N_COL, 8, 128), F32),
             dma((2, NCHUNK)),
             dma((6,)),
             dma((N_COL,)),
             dma((N_COL,)),
-            dma((5, N_OBS)),
-            dma((5, N_OBS)),
+            dma((1, N_OBS)),
+            dma((1, N_OBS)),
+            dma((3, len(K_PARTS))),
+            dma((3, len(K_PARTS))),
+            dma((4, GUESTS)),
+            dma((4, GUESTS)),
             dma((24,)),
             dma((24,)),
         ],

time: 59.1 us -> 53.3 us (0.902)
  Pallas kernels: 56.6 us -> 51.2 us
    pallas_call x1, Pallas kernels: 52.7 us -> 47.4 us  [per_device(): pl.pallas_call(inner_loop, out_shape=jax.ShapeDtypeStruct((2, SLOTS, FPAD...]
where the time goes in v3:
time: 53.3 us; the launch traced here: 53.2 us
  Pallas kernels  51.2 us (96%)
  between operations  1.93 us (4%)
    pallas_call x1, Pallas kernels, per_device(): pl.pallas_call(inner_loop, out_shape=jax.ShapeDtypeStruct((2, SLOTS, FPAD...  47.4 us
    pallas_call x1, Pallas kernels, per_device(): pl.pallas_call(expand, out_shape=(out, out), in_specs=[hbm], out_specs=(h...  3.85 us

profile of v3, /device:TPU:0, one launch (start us, length us, event | category | flops | bytes accessed | tf_op | source)
XLA Modules:
  0.0 53.2 jit_solution(6637284019217074984)
XLA Ops:
  1.9 47.4 %inner_loop.1.packed = bf16[2,256,640]{2,1,0:T(8,128)(2,1)} custom-call(s32[1]{0:T(128)S(6)} %copy.10.count_hbm, s32[1]{0:T(128)S(6)} %copy.11.channels_hbm, s32[1,128]{1,0:T(1,128)} %bitcast.6, s32[1,128]{1,0:T(1,128)} %bitcast.7, f32[1,4096]{1,0:T(1,128)} %error_hbm.1, f32[137,4,137]{2,1,0:T(4,128)} %bitcast.5, f32[128,4096]{1,0:T(8,128)} %dep_hbm.1, ...), custom_call_target="tpu_custom_call" | custom-call | tf_op jit(solution)/shard_map/inner_loop/pallas_call | solution.py:460
  49.3 3.8 %expand.1 = (f32[137,4,1024]{2,1,0:T(4,128)}, f32[137,4,1024]{2,1,0:T(4,128)}) custom-call(bf16[2,256,640]{2,1,0:T(8,128)(2,1)} %inner_loop.1.packed), custom_call_target="tpu_custom_call" | custom-call | tf_op jit(solution)/shard_map/expand/pallas_call | solution.py:509

commit v4 on v3

--- a/solution.py
+++ b/solution.py
@@ -44,7 +44,7 @@
 def inner_loop(
     count_hbm, channels_hbm, owner_hbm, column_hbm, error_hbm, vertical_hbm, dep_hbm, jac_hbm,
     out,
-    obs_count, channel_count, owner, column, error_inv, vertical, dep, jac, lift, lift_low, gram, gram_low, kern, kacc, racc,
+    obs_count, channel_count, owner, column, error_inv, vertical, dep, jac, lift, lift_low, gram, gram_low, kern, kacc,
     same, full1, wide, split, sent, held, queued, rows0, prof0, rows1, prof1, rows2, guest0, reply0, guest1, reply1, tile_a, tile_b,
     in_sem, small_sem, col_send, col_recv, obs_send, obs_recv, kern_send, kern_recv, leg_send, leg_recv, sum_send, sum_recv,
 ):
@@ -98,22 +98,31 @@
         channel = chunk * CHUNK + iota((1, CHUNK), 1)
         return jnp.where(channel < channel_count[0], error_inv[:, lanes], 0.0)
 
-    racc[...] = jnp.zeros_like(racc)
-
-    def rhs_chunk(chunk, carry):
+    kacc[...] = jnp.zeros_like(kacc)
+
+    def kern_chunk(chunk, top, acc):
+        count = min(256, FEAT - top)
+        scaled = (jac[chunk, top : top + count, :].astype(F32) * weights(chunk)).astype(BF)
+        acc[0 : FEAT - top, 0:count] += lax.dot_general(jac[chunk, top:FEAT, :], scaled, NT, preferred_element_type=F32)
+
+    def first_chunk(chunk, carry):
         for copy in load(chunk):
             copy.wait()
-        weighted = (weights(chunk) * dep[chunk]).astype(BF)
-        racc[:, 0:FEAT] += lax.dot_general(weighted, jac[chunk], NT, preferred_element_type=F32)
+        weight = weights(chunk)
+        beside = jnp.concatenate(
+            [(jac[chunk, 0:256, :].astype(F32) * weight).astype(BF), (weight * dep[chunk]).astype(BF)], axis=0
+        )
+        kacc[0:FEAT, :] += lax.dot_general(jac[chunk], beside, NT, preferred_element_type=F32)
         return carry
 
-    lax.fori_loop(0, NCHUNK, rhs_chunk, 0)
-    lane = iota((ROWS, FPAD), 1)
-    rows = racc[...]
-    rows = jnp.where(lane == FEAT, column_high, rows)
-    rows = jnp.where(lane == FEAT + 1, column_low, rows)
-    rows = jnp.where(lane == FEAT + 2, 1.0, rows)
-    sent[...] = jnp.dot(place, rows.astype(BF), preferred_element_type=F32).astype(BF)
+    lax.fori_loop(0, NCHUNK, first_chunk, 0)
+    lane = iota((ROWS, 128), 1)
+    extras = jnp.where(lane == FEAT - 512, column_high, 0.0)
+    extras = jnp.where(lane == FEAT + 1 - 512, column_low, extras)
+    extras = jnp.where(lane == FEAT + 2 - 512, 1.0, extras).astype(BF)
+    placed = lax.dot_general(place, kacc[:, 256:384].astype(BF), NT, preferred_element_type=F32)
+    tail = placed[:, 512:640] + jnp.dot(place, extras, preferred_element_type=F32)
+    sent[...] = jnp.concatenate([placed[:, 0:512], tail], axis=1).astype(BF)
 
     pl.semaphore_wait(barrier, N_OBS - 1 + N_COL - 1)
 
@@ -134,51 +143,47 @@
     for first, count in K_FREE:
         kern[:, first : first + count, :] = jnp.zeros((3, count, 256), BF)
     kern_copies = []
-    diagonal = iota((128, 128), 0) == iota((128, 128), 1)
+    diagonal = iota((256, 256), 0) == iota((256, 256), 1)
 
     def kern_part(which, index):
         first, count, lane_at = K_PARTS[index]
         return kern.at[which, pl.ds(first, count), pl.ds(lane_at, 128)]
 
-    def make_kern(index, shift):
-        first, count, lane_at = K_PARTS[index]
-        lanes = slice(lane_at, lane_at + 128)
-        top = index * 128
-        wide_rows = min(128, FEAT - top)
-        kacc[...] = jnp.zeros_like(kacc)
-
-        def kern_chunk(chunk, carry):
-            scaled = (jac[chunk, top : top + wide_rows, :].astype(F32) * weights(chunk)).astype(BF)
-            kacc[0 : FEAT - top, 0:wide_rows] += lax.dot_general(
-                jac[chunk, top:FEAT, :], scaled, NT, preferred_element_type=F32
-            )
-            return carry
-
-        lax.fori_loop(0, NCHUNK, kern_chunk, 0)
-        if index == 0:
-            shift = (total(jnp.where(diagonal, kacc[0:128], 0.0)) * (1.0 / 128)).astype(BF).astype(F32)
-        if wide_rows < 128:
-            corner = jnp.where(diagonal, kacc[0:128] - shift, kacc[0:128])
-            kern[1, first : first + count, lanes] = jnp.where(iota((128, 128), 0) < wide_rows, corner, shift)[0:count].astype(BF)
-        else:
-            kern[1, first : first + 128, lanes] = jnp.where(diagonal, kacc[0:128] - shift, kacc[0:128]).astype(BF)
-            kern[1, first + 128 : first + count, lanes] = kacc[128:count].astype(BF)
-        for target, away in ((0, 1), (2, 3)):
-            copy = pltpu.make_async_remote_copy(
-                src_ref=kern_part(1, index), dst_ref=kern_part(target, index),
-                send_sem=kern_send.at[target, index], recv_sem=kern_recv.at[target, index],
-                device_id={"obs": lax.rem(chip + away, N_CHIP) * 2 + core}, device_id_type=MESH,
-            )
-            copy.start()
-            kern_copies.append(copy)
-        return shift
+    def send_kern(parts):
+        for index in parts:
+            for target, away in ((0, 1), (2, 3)):
+                copy = pltpu.make_async_remote_copy(
+                    src_ref=kern_part(1, index), dst_ref=kern_part(target, index),
+                    send_sem=kern_send.at[target, index], recv_sem=kern_recv.at[target, index],
+                    device_id={"obs": lax.rem(chip + away, N_CHIP) * 2 + core}, device_id_type=MESH,
+                )
+                copy.start()
+                kern_copies.append(copy)
 
     def fill_kern(which):
         for first in (0, 640):
             kern[which, first : first + 128, 128:256] = kern[which, first + 128 : first + 256, 0:128].astype(F32).T.astype(BF)
 
-    shift = make_kern(0, None)
-    make_kern(1, shift)
+    corner = kacc[0:256, 0:256]
+    shift = (total(jnp.where(diagonal, corner, 0.0)) * (1.0 / 256)).astype(BF).astype(F32)
+    kern[1, 0:256, :] = jnp.where(diagonal, corner - shift, corner).astype(BF)
+    kern[1, 256:560, :] = kacc[256:560, 0:256].astype(BF)
+    send_kern((0, 1))
+    for first, top in ((640, 256), (1024, 512)):
+        kacc[0:304, 0:256] = jnp.zeros((304, 256), F32)
+
+        def more_chunk(chunk, carry):
+            kern_chunk(chunk, top, kacc)
+            return carry
+
+        lax.fori_loop(0, NCHUNK, more_chunk, 0)
+        corner = kacc[0:256, 0:256]
+        corner = jnp.where(diagonal, corner - shift, corner)
+        if top == 256:
+            kern[1, first : first + 256, :] = corner.astype(BF)
+            kern[1, first + 256 : first + 304, :] = kacc[256:304, 0:256].astype(BF)
+        else:
+            kern[1, first : first + 48, 0:128] = jnp.where(iota((48, 128), 0) < FEAT - top, corner[0:48, 0:128], shift).astype(BF)
 
     for copy in col_copies:
         copy.wait_recv()
@@ -219,9 +224,7 @@
 
     for away in (*CHIP_ORDER, 0):
         rows_to(0, away, queued, rows0)
-    for index in (2, 3, 4):
-        make_kern(index, shift)
-    fill_kern(1)
+    send_kern((2, 3, 4))
     lift[...] = jnp.zeros_like(lift)
     small[0].wait()
     for var in range(NVAR):
@@ -269,6 +272,7 @@
         split[0] = high
         split[1] = low
         moment = jnp.zeros((1, 1), F32)
+        products = []
         for away in (*CHIP_ORDER, 0):
             here = block(lax.rem(chip + away, N_CHIP), CHIP_ROWS)
             pair = jnp.concatenate([split[0, here, :], split[1, here, :]], axis=0)
@@ -276,6 +280,8 @@
             lifted = both[0:CHIP_ROWS] + both[CHIP_ROWS:]
             prof_ref[here, :] = lifted.astype(BF)
             profiles_to(number, away, prof_ref, target_ref)
+            products.append((lifted, here))
+        for lifted, here in products:
             moment += total(lifted * own[here, :].astype(F32))
         return moment
 
@@ -331,19 +337,26 @@
             )
             away_shift = kern[which, 1056:1072, 0:128].astype(F32)[8:9, 0:1]
             rows_out = jnp.where(iota(adjoint.shape, 1) == FEAT, away_shift, adjoint).astype(BF)
-            profiles = profiles.astype(F32)
-            moment += total(profiles * (adjoint + away_shift * profiles))
             target_ref[own, :] = rows_out[0:OBS_ROWS]
             for index, guest in enumerate(guests):
                 reply_ref[guest] = rows_out[(index + 1) * OBS_ROWS : (index + 2) * OBS_ROWS]
-            if after is not None and which == 2:
+
+            def answer():
+                for guest in guests:
+                    if guest < 3:
+                        go(copy_of(number + 1, reply_ref.at[guest], target_ref.at[own], guest, guest, sibling))
+                    else:
+                        back = lax.rem(chip + (1 if guest == 3 else 3), N_CHIP) * 2 + (1 if guest == 3 else 0)
+                        go(copy_of(number + 1, reply_ref.at[guest], target_ref.at[own], guest, 3 + core, back))
+
+            last = after is not None and which == 2
+            if not last:
+                answer()
+            profiles = profiles.astype(F32)
+            moment += total(profiles * (adjoint + away_shift * profiles))
+            if last:
                 after(moment)
-            for guest in guests:
-                if guest < 3:
-                    go(copy_of(number + 1, reply_ref.at[guest], target_ref.at[own], guest, guest, sibling))
-                else:
-                    back = lax.rem(chip + (1 if guest == 3 else 3), N_CHIP) * 2 + (1 if guest == 3 else 0)
-                    go(copy_of(number + 1, reply_ref.at[guest], target_ref.at[own], guest, 3 + core, back))
+                answer()
         return moment
 
     def replies(number, target_ref):
@@ -476,8 +489,7 @@
             pltpu.VMEM((FPAD, FPAD), F32),
             pltpu.VMEM((FPAD, FPAD), BF),
             pltpu.VMEM((3, K_ROWS, 256), BF),
-            pltpu.VMEM((FPAD, 128), F32),
-            pltpu.VMEM((ROWS, FPAD), F32),
+            pltpu.VMEM((FPAD, 384), F32),
             pltpu.VMEM((SLOTS, SLOTS), BF),
             pltpu.VMEM((SLOTS, FPAD), F32),
             pltpu.VMEM((3, SLOTS, FPAD), F32),

time: 53.3 us -> 52.1 us (0.977)
  Pallas kernels: 51.2 us -> 50 us
    pallas_call x1, Pallas kernels: 47.4 us -> 46.1 us  [per_device(): pl.pallas_call(inner_loop, out_shape=jax.ShapeDtypeStruct((2, SLOTS, FPAD...]
where the time goes in v4:
time: 52.1 us; the launch traced here: 51.9 us
  Pallas kernels  50 us (96%)
  between operations  1.93 us (4%)
    pallas_call x1, Pallas kernels, per_device(): pl.pallas_call(inner_loop, out_shape=jax.ShapeDtypeStruct((2, SLOTS, FPAD...  46.1 us
    pallas_call x1, Pallas kernels, per_device(): pl.pallas_call(expand, out_shape=(out, out), in_specs=[hbm], out_specs=(h...  3.86 us

profile of v4, /device:TPU:0, one launch (start us, length us, event | category | flops | bytes accessed | tf_op | source)
XLA Modules:
  0.0 51.9 jit_solution(2474201405076293229)
XLA Ops:
  1.9 46.1 %inner_loop.1.packed = bf16[2,256,640]{2,1,0:T(8,128)(2,1)} custom-call(s32[1]{0:T(128)S(6)} %copy.10.count_hbm, s32[1]{0:T(128)S(6)} %copy.11.channels_hbm, s32[1,128]{1,0:T(1,128)} %bitcast.6, s32[1,128]{1,0:T(1,128)} %bitcast.7, f32[1,4096]{1,0:T(1,128)} %error_hbm.1, f32[137,4,137]{2,1,0:T(4,128)} %bitcast.5, f32[128,4096]{1,0:T(8,128)} %dep_hbm.1, ...), custom_call_target="tpu_custom_call" | custom-call | tf_op jit(solution)/shard_map/inner_loop/pallas_call | solution.py:473
  48.1 3.9 %expand.1 = (f32[137,4,1024]{2,1,0:T(4,128)}, f32[137,4,1024]{2,1,0:T(4,128)}) custom-call(bf16[2,256,640]{2,1,0:T(8,128)(2,1)} %inner_loop.1.packed), custom_call_target="tpu_custom_call" | custom-call | tf_op jit(solution)/shard_map/expand/pallas_call | solution.py:521

commit v5 on v4

--- a/solution.py
+++ b/solution.py
@@ -110,7 +110,7 @@
             copy.wait()
         weight = weights(chunk)
         beside = jnp.concatenate(
-            [(jac[chunk, 0:256, :].astype(F32) * weight).astype(BF), (weight * dep[chunk]).astype(BF)], axis=0
+            [(jac[chunk, 0:128, :].astype(F32) * weight).astype(BF), (weight * dep[chunk]).astype(BF)], axis=0
         )
         kacc[0:FEAT, :] += lax.dot_general(jac[chunk], beside, NT, preferred_element_type=F32)
         return carry
@@ -120,7 +120,7 @@
     extras = jnp.where(lane == FEAT - 512, column_high, 0.0)
     extras = jnp.where(lane == FEAT + 1 - 512, column_low, extras)
     extras = jnp.where(lane == FEAT + 2 - 512, 1.0, extras).astype(BF)
-    placed = lax.dot_general(place, kacc[:, 256:384].astype(BF), NT, preferred_element_type=F32)
+    placed = lax.dot_general(place, kacc[:, 128:256].astype(BF), NT, preferred_element_type=F32)
     tail = placed[:, 512:640] + jnp.dot(place, extras, preferred_element_type=F32)
     sent[...] = jnp.concatenate([placed[:, 0:512], tail], axis=1).astype(BF)
 
@@ -164,26 +164,34 @@
         for first in (0, 640):
             kern[which, first : first + 128, 128:256] = kern[which, first + 128 : first + 256, 0:128].astype(F32).T.astype(BF)
 
-    corner = kacc[0:256, 0:256]
-    shift = (total(jnp.where(diagonal, corner, 0.0)) * (1.0 / 256)).astype(BF).astype(F32)
-    kern[1, 0:256, :] = jnp.where(diagonal, corner - shift, corner).astype(BF)
-    kern[1, 256:560, :] = kacc[256:560, 0:256].astype(BF)
-    send_kern((0, 1))
-    for first, top in ((640, 256), (1024, 512)):
-        kacc[0:304, 0:256] = jnp.zeros((304, 256), F32)
+    corner = kacc[0:128, 0:128]
+    diagonal_low = diagonal[0:128, 0:128]
+    shift = (total(jnp.where(diagonal_low, corner, 0.0)) * (1.0 / 128)).astype(BF).astype(F32)
+    kern[1, 0:128, 0:128] = jnp.where(diagonal_low, corner - shift, corner).astype(BF)
+    kern[1, 128:560, 0:128] = kacc[128:560, 0:128].astype(BF)
+    send_kern((0,))
+    for top, rows_here in ((128, 432), (384, 176)):
+        kacc[0:rows_here] = jnp.zeros((rows_here, 256), F32)
 
         def more_chunk(chunk, carry):
             kern_chunk(chunk, top, kacc)
             return carry
 
         lax.fori_loop(0, NCHUNK, more_chunk, 0)
-        corner = kacc[0:256, 0:256]
-        corner = jnp.where(diagonal, corner - shift, corner)
-        if top == 256:
-            kern[1, first : first + 256, :] = corner.astype(BF)
-            kern[1, first + 256 : first + 304, :] = kacc[256:304, 0:256].astype(BF)
+        if top == 128:
+            corner = kacc[0:256]
+            corner = jnp.where(diagonal, corner - shift, corner).astype(BF)
+            kern[1, 128:384, 128:256] = corner[:, 0:128]
+            kern[1, 384:560, 128:256] = kacc[256:432, 0:128].astype(BF)
+            kern[1, 640:768, 0:128] = corner[128:256, 128:256]
+            kern[1, 768:944, 0:128] = kacc[256:432, 128:256].astype(BF)
+            send_kern((1,))
         else:
-            kern[1, first : first + 48, 0:128] = jnp.where(iota((48, 128), 0) < FEAT - top, corner[0:48, 0:128], shift).astype(BF)
+            corner = kacc[0:176]
+            corner = jnp.where(diagonal[0:176], corner - shift, corner)
+            kern[1, 768:944, 128:256] = corner[:, 0:128].astype(BF)
+            kern[1, 1024:1072, 0:128] = jnp.where(iota((48, 128), 0) < FEAT - 512, corner[128:176, 128:256], shift).astype(BF)
+    fill_kern(1)
 
     for copy in col_copies:
         copy.wait_recv()
@@ -489,7 +497,7 @@
             pltpu.VMEM((FPAD, FPAD), F32),
             pltpu.VMEM((FPAD, FPAD), BF),
             pltpu.VMEM((3, K_ROWS, 256), BF),
-            pltpu.VMEM((FPAD, 384), F32),
+            pltpu.VMEM((FPAD, 256), F32),
             pltpu.VMEM((SLOTS, SLOTS), BF),
             pltpu.VMEM((SLOTS, FPAD), F32),
             pltpu.VMEM((3, SLOTS, FPAD), F32),

time: 52.1 us -> 50.9 us (0.977)
  Pallas kernels: 50 us -> 48.8 us
    pallas_call x1, Pallas kernels: 46.1 us -> 45 us  [per_device(): pl.pallas_call(inner_loop, out_shape=jax.ShapeDtypeStruct((2, SLOTS, FPAD...]
where the time goes in v5:
time: 50.9 us; the launch traced here: 50.7 us
  Pallas kernels  48.8 us (96%)
  between operations  1.93 us (4%)
    pallas_call x1, Pallas kernels, per_device(): pl.pallas_call(inner_loop, out_shape=jax.ShapeDtypeStruct((2, SLOTS, FPAD...  45 us
    pallas_call x1, Pallas kernels, per_device(): pl.pallas_call(expand, out_shape=(out, out), in_specs=[hbm], out_specs=(h...  3.85 us

profile of v5, /device:TPU:0, one launch (start us, length us, event | category | flops | bytes accessed | tf_op | source)
XLA Modules:
  0.0 50.7 jit_solution(11986168684473822271)
XLA Ops:
  1.9 45.0 %inner_loop.1.packed = bf16[2,256,640]{2,1,0:T(8,128)(2,1)} custom-call(s32[1]{0:T(128)S(6)} %copy.10.count_hbm, s32[1]{0:T(128)S(6)} %copy.11.channels_hbm, s32[1,128]{1,0:T(1,128)} %bitcast.6, s32[1,128]{1,0:T(1,128)} %bitcast.7, f32[1,4096]{1,0:T(1,128)} %error_hbm.1, f32[137,4,137]{2,1,0:T(4,128)} %bitcast.5, f32[128,4096]{1,0:T(8,128)} %dep_hbm.1, ...), custom_call_target="tpu_custom_call" | custom-call | tf_op jit(solution)/shard_map/inner_loop/pallas_call | solution.py:481
  46.9 3.8 %expand.1 = (f32[137,4,1024]{2,1,0:T(4,128)}, f32[137,4,1024]{2,1,0:T(4,128)}) custom-call(bf16[2,256,640]{2,1,0:T(8,128)(2,1)} %inner_loop.1.packed), custom_call_target="tpu_custom_call" | custom-call | tf_op jit(solution)/shard_map/expand/pallas_call | solution.py:529

commit v6 on v5

--- a/solution.py
+++ b/solution.py
@@ -46,7 +46,7 @@
     out,
     obs_count, channel_count, owner, column, error_inv, vertical, dep, jac, lift, lift_low, gram, gram_low, kern, kacc,
     same, full1, wide, split, sent, held, queued, rows0, prof0, rows1, prof1, rows2, guest0, reply0, guest1, reply1, tile_a, tile_b,
-    in_sem, small_sem, col_send, col_recv, obs_send, obs_recv, kern_send, kern_recv, leg_send, leg_recv, sum_send, sum_recv,
+    in_sem, small_sem, col_send, col_recv, obs_send, obs_recv, kern_send, kern_recv, leg_send, leg_recv, sum_send, sum_recv, ready, out_sem,
 ):
     col, obs = lax.axis_index("col"), lax.axis_index("obs")
     chip, core = obs // 2, lax.rem(obs, 2)
@@ -434,13 +434,18 @@
     curve = dir0 * dir0 * m0 + (dir0 * (dir0 + dir1) + dir0 * dir1) * m1 + (dir0 * dir1 + dir1 * (dir0 + dir1)) * m2 + dir1 * dir1 * m3
     step1 = norm1 / curve
     tail = iota((SLOTS, FPAD), 1) >= FEAT
+    stores = [pltpu.make_async_copy(ready.at[half], out.at[half], out_sem.at[half]) for half in range(2)]
     inc = (step0 + step1 * dir0) * wide[0] + (step1 * dir1) * wide[1]
+    ready[0] = jnp.where(tail, rows0[...].astype(F32), inc).astype(BF)
+    stores[0].start()
     res = (rest - step1 * dir0) * wide[0] - (step0 + step1 * (dir0 + dir1)) * wide[1] - (step1 * dir1) * wide[2]
-    out[0] = jnp.where(tail, rows0[...].astype(F32), inc).astype(BF)
-    out[1] = jnp.where(tail, 0.0, res).astype(BF)
+    ready[1] = jnp.where(tail, 0.0, res).astype(BF)
+    stores[1].start()
 
     for copy in (*col_copies, *kern_copies, *sends, *sums, *sums_col):
         copy.wait_send()
+    for store in stores:
+        store.wait()
 
 
 def expand(packed, out_inc, out_res, taken, full_inc, full_res, in_sem, out_sem):
@@ -482,7 +487,7 @@
         inner_loop,
         out_shape=jax.ShapeDtypeStruct((2, SLOTS, FPAD), BF),
         in_specs=[hbm] * 8,
-        out_specs=vmem,
+        out_specs=hbm,
         scratch_shapes=[
             pltpu.SMEM((1,), jnp.int32),
             pltpu.SMEM((1,), jnp.int32),
@@ -518,6 +523,8 @@
             dma((4, GUESTS)),
             dma((24,)),
             dma((24,)),
+            pltpu.VMEM((2, SLOTS, FPAD), BF),
+            dma((2,)),
         ],
         compiler_params=pltpu.CompilerParams(collective_id=0, has_side_effects=True, vmem_limit_bytes=62 << 20),
         name="inner_loop",

time: 50.9 us -> 50.7 us (level)
  no operation moved by 1% of the time
where the time goes in v6:
time: 50.7 us; the launch traced here: 50.5 us
  Pallas kernels  48.6 us (96%)
  between operations  1.93 us (4%)
    pallas_call x1, Pallas kernels, per_device(): pl.pallas_call(inner_loop, out_shape=jax.ShapeDtypeStruct((2, SLOTS, FPAD...  44.7 us
    pallas_call x1, Pallas kernels, per_device(): pl.pallas_call(expand, out_shape=(out, out), in_specs=[hbm], out_specs=(h...  3.85 us

profile of v6, /device:TPU:0, one launch (start us, length us, event | category | flops | bytes accessed | tf_op | source)
XLA Modules:
  0.0 50.5 jit_solution(5531905638000821272)
XLA Ops:
  1.9 44.7 %inner_loop.1.packed = bf16[2,256,640]{2,1,0:T(8,128)(2,1)} custom-call(s32[1]{0:T(128)S(6)} %copy.10.count_hbm, s32[1]{0:T(128)S(6)} %copy.11.channels_hbm, s32[1,128]{1,0:T(1,128)} %bitcast.6, s32[1,128]{1,0:T(1,128)} %bitcast.7, f32[1,4096]{1,0:T(1,128)} %error_hbm.1, f32[137,4,137]{2,1,0:T(4,128)} %bitcast.5, f32[128,4096]{1,0:T(8,128)} %dep_hbm.1, ...), custom_call_target="tpu_custom_call" | custom-call | tf_op jit(solution)/shard_map/inner_loop/pallas_call | solution.py:486
  46.7 3.8 %expand.1 = (f32[137,4,1024]{2,1,0:T(4,128)}, f32[137,4,1024]{2,1,0:T(4,128)}) custom-call(bf16[2,256,640]{2,1,0:T(8,128)(2,1)} %inner_loop.1.packed), custom_call_target="tpu_custom_call" | custom-call | tf_op jit(solution)/shard_map/expand/pallas_call | solution.py:536
